TPU v7x, 256 devices: a whole 4x4x8 slice. The times are simulated.
256 devices in a mesh: kv: 64 (over y, z, core), tp: 4 (over x).
Axes of the slice: x: 4, y: 4, z: 8, core: 2. Of those that a mesh axis runs over, the one named last changes fastest.
Arguments:
- query: bfloat16 [16, 128, 128], P(None, 'tp'), may hold values from -128 to 128
- key_cache: bfloat16 [16, 32768, 8, 128], P(None, 'kv', 'tp'), may hold values from -4 to 4
- value_cache: bfloat16 [16, 32768, 8, 128], P(None, 'kv', 'tp'), may hold values from -6 to 6
- lengths: int32 [16], replicated, may hold values from 4096 to 32768, as said below
- out_weight: bfloat16 [128, 128, 16384], P('tp', 'kv'), may hold values from -0.046875 to 0.046875
Outputs:
- projected: bfloat16 [16, 16384], P(None, ('kv', 'tp'))
Inputs may be any that keep to these rules, and one draw needn't show every extreme that they name: lengths[0] is 32768.
All inputs are finite; a program needn't handle non-finite values.
Results may differ from a plain program's by a relative error of at most 0.007.
Values may be sent and summed in bfloat16 or wider, within the bound.
No kernel may reach another device: no remote copies, remote signals or barrier semaphores. Data moves between devices by JAX's collectives and lax.ppermute only.
A program may use at most 128 MiB of HBM per device.

v0:
```python
import jax
import jax.numpy as jnp
from jax import lax
from jax.sharding import PartitionSpec as P


def local(query, key_cache, value_cache, lengths, out_weight):
    batch, local_heads, head_size = query.shape
    positions_dev = key_cache.shape[1]
    local_kv = key_cache.shape[2]
    group = local_heads // local_kv
    kv_count = lax.axis_size("kv")
    kv_index = lax.axis_index("kv")
    positions = kv_index * positions_dev + jnp.arange(positions_dev, dtype=jnp.int32)
    live = (positions[None, :] < lengths[:, None])[:, None, None, :]
    grouped = query.reshape(batch, local_kv, group, head_size)
    scores = jnp.einsum("bgqd,bpgd->bgqp", grouped, key_cache, preferred_element_type=jnp.float32)
    scores = scores / jnp.sqrt(jnp.float32(head_size))
    masked = jnp.where(live, scores, jnp.float32(-1e30))
    block_max = jnp.max(masked, axis=-1)
    weights = jnp.where(live, jnp.exp(scores - block_max[..., None]), jnp.float32(0.0))
    block_total = jnp.sum(weights, axis=-1)
    weight_bf = weights.astype(jnp.bfloat16)
    summed = jnp.einsum(
        "bgqp,bpgd->bgqd", weight_bf, value_cache, preferred_element_type=jnp.float32
    )
    floored = jnp.maximum(block_total, jnp.float32(1.0))
    block_out = (
        (summed / floored[..., None]).astype(jnp.bfloat16).reshape(batch, local_heads, head_size)
    )
    block_lse = (block_max + jnp.log(floored)).reshape(batch, local_heads)
    feature_width = head_size // kv_count
    pieces = lax.all_to_all(block_out[None], "kv", split_axis=3, concat_axis=0, tiled=True)
    lse_rows = lax.all_gather(block_lse[None], "kv", axis=0, tiled=True)
    highest = jnp.max(lse_rows, axis=0)
    scales = jnp.exp(lse_rows - highest[None])
    merged = (
        jnp.sum(scales[..., None] * pieces.astype(jnp.float32), axis=0)
        / jnp.sum(scales, axis=0)[..., None]
    )
    merged_bf = merged.astype(jnp.bfloat16).reshape(batch, local_heads * feature_width)
    width = out_weight.shape[2]
    terms = jnp.dot(
        merged_bf,
        out_weight.reshape(local_heads * feature_width, width),
        preferred_element_type=jnp.float32,
    )
    result = lax.psum_scatter(terms, ("kv", "tp"), scatter_dimension=1, tiled=True)
    return result.astype(jnp.bfloat16)


def solution(mesh):
    placed = (
        P(None, "tp", None),
        P(None, "kv", "tp", None),
        P(None, "kv", "tp", None),
        P(),
        P("tp", "kv", None),
    )
    return jax.shard_map(
        local, mesh=mesh, in_specs=placed, out_specs=P(None, ("kv", "tp")), check_vma=False
    )
```

profile of v0, /device:TPU:1, one launch (start us, length us, event | category | flops | bytes accessed | tf_op | source)
XLA Modules:
  0.0 1368.6 jit_solution(10125151176008989673)
XLA Ops:
  6.5 0.0 copy-start
  6.5 0.0 copy-start.1
  6.5 0.9 broadcast_compare_fusion
  7.4 3.9 select_reduce_fusion
  11.3 0.4 fusion.16
  11.8 0.0 copy-done.1
  11.8 0.8 fusion.11
  12.6 0.4 copy.16
  13.1 1.1 reshape.76
  14.1 13.2 all-to-all-start
  27.3 0.0 reduce-scatter.4.cloned.1.call-start
  27.3 0.1 add.28
  27.4 51.1 %all_gather.3 = f32[64,16,32]{2,1,0:T(8,128)S(1)} all-gather(f32[1,16,32]{2,1,0:T(8,128)S(1)} %add.28), channel_id=1, replica_groups=mesh['kv'=64,'tp'=4] {'kv'}, dimensions={0}, use_global_device_ids=true | all-gather | bytes 133120 | tf_op jit(solution)/shard_map/all_gather | solution.py:34
  78.6 0.1 reduce_max.19
  78.6 0.1 fusion.23
  78.8 0.0 all-to-all-done
  78.8 0.3 reshape.77
  79.1 0.2 fusion.14
  79.2 0.0 copy-done
  79.2 6.9 convolution_bitcast_fusion
  86.2 0.0 reduce-scatter.4.cloned.1.call-update
  86.2 1274.2 %reduce-scatter.4.cloned.1.call-done = f32[64,16]{1,0:T(8,128)} async-done(((f32[16384,16]{1,0:T(8,128)}), f32[64,16]{1,0:T(8,128)}) %reduce-scatter.4.cloned.1.call-update) | async-done | bytes 4112
  1360.4 1.4 copy.19
  (2 shorter events, 0.0 us)
Async XLA Ops:
  6.5 72.7 %copy-start = (bf16[32,2,16384]{2,1,0:T(2,128)(2,1)S(1)}, bf16[32,2,16384]{2,1,0:T(2,128)(2,1)}, u32[]{:S(2)}) copy-start(bf16[32,2,16384]{2,1,0:T(2,128)(2,1)} %param.9) | copy-start | bytes 6291460
  6.5 5.2 copy-start.1
  14.1 64.6 %all-to-all-start = ((bf16[64,2,512]{2,1,0:T(2,128)(2,1)}), bf16[64,2,512]{2,1,0:T(2,128)(2,1)S(1)}, u32[]{:S(2)}, u32[]{:S(2)}) async-start(bf16[64,2,512]{2,1,0:T(2,128)(2,1)} %reshape.76), calls=%async_computation | async-start | bytes 262144 | tf_op jit(solution)/shard_map/all_to_all | solution.py:33
  27.3 1333.1 %reduce-scatter.4.cloned.1.call-start = ((), (), s32[]{:S(2)}) async-start(), calls=%async_computation.2 | async-start | bytes 8421376
Sparse Core Ops, SparseCore 0:
  86.3 1274.0 reduce-scatter.3
where the time goes:
time: 1370 us
  waiting for transfers between devices  1270 us (93%)
  blocking collectives  51.1 us (4%)
    unnamed x2, waiting for transfers between devices  1270 us
    all_gather x1, blocking collectives, local(): lse_rows = lax.all_gather(block_lse[None], 'kv', axis=0, tiled=True)  51.1 us
  transfers between devices with their start and end apart: 2, of which 1 were waited for; matrix products, arithmetic and copies ran while one was open for 0% of the time, Pallas kernels for 0%

commit v1 on v0

v1 whole, which is shorter than its diff:
```python
import functools

import jax
import jax.numpy as jnp
import numpy as np
from jax import lax
from jax.experimental import pallas as pl
from jax.experimental.pallas import tpu as pltpu
from jax.sharding import Mesh
from jax.sharding import PartitionSpec as P

SEQS = 16
HEADS = 32
LANES = 128
CHIP_FEATURES = 4
HALF = 8192


def spread_table():
    table = np.zeros((CHIP_FEATURES, 4, HEADS, LANES), np.float32)
    for i in range(CHIP_FEATURES):
        for h in range(HEADS):
            table[i, :, h, (i // 2) * 64 + h * 2 + i % 2] = 1.0
    return table.reshape(4 * LANES, LANES)


def repeat_table():
    table = np.zeros((4, 4, 4, 16), np.float32)
    for i in range(4):
        for k in range(4):
            table[i, k, :, i * 4 + k] = 1.0
    return table.reshape(64, 16)


def merge_project_kernel(got_ref, weight_ref, spread_ref, repeat_ref, out_ref):
    got = got_ref[...].astype(jnp.float32).reshape(64, 24, LANES)
    stats = got[:, 16:24]
    swapped = pltpu.roll(stats, 4, 1)
    upper = lax.broadcasted_iota(jnp.int32, stats.shape, 1) < 4
    coarse = jnp.where(upper, stats, swapped)
    fine = jnp.where(upper, swapped, stats)
    scale = jnp.exp(coarse - jnp.max(coarse, axis=0, keepdims=True))
    total = jnp.sum(scale * fine, axis=0)
    first = jnp.sum(scale * got[:, 0:8], axis=0) / total
    second = jnp.sum(scale * got[:, 8:16], axis=0) / total
    merged = jnp.concatenate([first, second], axis=0).astype(jnp.bfloat16)
    rows = jnp.dot(repeat_ref[...], merged, preferred_element_type=jnp.float32)
    lane_group = lax.broadcasted_iota(jnp.int32, rows.shape, 1) // 32
    row_group = lax.broadcasted_iota(jnp.int32, rows.shape, 0) % 4
    rows = jnp.where(lane_group == row_group, rows, 0.0).astype(jnp.bfloat16)
    wide = jnp.concatenate([rows[16 * i : 16 * i + 16] for i in range(4)], axis=1)
    left = jnp.dot(wide, spread_ref[...], preferred_element_type=jnp.float32).astype(jnp.bfloat16)
    low = lax.broadcasted_iota(jnp.int32, (8, LANES), 1) < 64
    step = 1024
    for start in range(0, HALF, step):
        part = jnp.dot(
            left, weight_ref[:, start : start + step], preferred_element_type=jnp.float32
        )
        for tile in range(step // LANES):
            piece = part[:, tile * LANES : (tile + 1) * LANES]
            top, bottom = piece[0:8], piece[8:16]
            even = jnp.where(low, top, pltpu.roll(bottom, 64, 1))
            odd = jnp.where(low, pltpu.roll(top, 64, 1), bottom)
            out_ref[start // LANES + tile] = jnp.concatenate([even, odd], axis=0).astype(
                jnp.bfloat16
            )


def merge_project(got, weight):
    vmem = pl.BlockSpec(memory_space=pltpu.VMEM)
    return pl.pallas_call(
        merge_project_kernel,
        out_shape=jax.ShapeDtypeStruct((HALF // LANES, 16, LANES), jnp.bfloat16),
        in_specs=[vmem] * 4,
        out_specs=vmem,
        compiler_params=pltpu.CompilerParams(vmem_limit_bytes=24 * 1024 * 1024),
        cost_estimate=pl.CostEstimate(flops=34_000_000, bytes_accessed=3_000_000, transcendentals=65536),
    )(
        got,
        weight,
        jnp.asarray(spread_table(), jnp.bfloat16),
        jnp.asarray(repeat_table(), jnp.bfloat16),
    )


def final_sum_kernel(got_ref, out_ref):
    total = jnp.sum(got_ref[...].astype(jnp.float32), axis=0)
    total = total[0:8] + total[8:16]
    out_ref[...] = jnp.concatenate([total[:, 0:64], total[:, 64:128]], axis=0).astype(jnp.bfloat16)


def final_sum(got):
    vmem = pl.BlockSpec(memory_space=pltpu.VMEM)
    return pl.pallas_call(
        final_sum_kernel,
        out_shape=jax.ShapeDtypeStruct((SEQS, 64), jnp.bfloat16),
        in_specs=[vmem],
        out_specs=vmem,
        compiler_params=pltpu.CompilerParams(vmem_limit_bytes=16 * 1024 * 1024),
        cost_estimate=pl.CostEstimate(flops=131072, bytes_accessed=264192, transcendentals=0),
    )(got)


def attend(query, key_cache, value_cache, lengths, block_index):
    batch, local_heads, head_size = query.shape
    positions_dev = key_cache.shape[1]
    local_kv = key_cache.shape[2]
    group = local_heads // local_kv
    positions = block_index * positions_dev + jnp.arange(positions_dev, dtype=jnp.int32)
    live = (positions[None, :] < lengths[:, None])[:, None, None, :]
    grouped = query.reshape(batch, local_kv, group, head_size)
    scores = jnp.einsum("bgqd,bpgd->bgqp", grouped, key_cache, preferred_element_type=jnp.float32)
    scores = scores * jnp.float32(head_size**-0.5)
    masked = jnp.where(live, scores, jnp.float32(-1e30))
    block_max = jnp.max(masked, axis=-1)
    weights = jnp.where(live, jnp.exp(scores - block_max[..., None]), jnp.float32(0.0))
    block_total = jnp.sum(weights, axis=-1)
    summed = jnp.einsum(
        "bgqp,bpgd->bgqd",
        weights.astype(jnp.bfloat16),
        value_cache,
        preferred_element_type=jnp.float32,
    )
    floored = jnp.maximum(block_total, jnp.float32(1.0))
    coarse = lax.reduce_precision(block_max + jnp.log(floored), 8, 7)
    some = block_total > 0
    fine = jnp.where(some, floored * jnp.exp(jnp.where(some, block_max - coarse, 0.0)), 0.0)
    fine = lax.reduce_precision(fine, 8, 7)
    scaled = (summed * (fine / floored)[..., None]).astype(jnp.bfloat16)
    features = scaled.reshape(batch * local_heads, head_size).T.reshape(32, 16, LANES)
    stats = jnp.concatenate([coarse.reshape(4, LANES), fine.reshape(4, LANES)]).astype(jnp.bfloat16)
    stats = jnp.broadcast_to(stats[None], (32, 8, LANES))
    return jnp.concatenate([features, stats], axis=1)


def local(query, key_cache, value_cache, lengths, out_weight):
    core = lax.axis_index("core")
    block_index = lax.axis_index("chip") * 2 + core
    packed = attend(query, key_cache, value_cache, lengths, block_index)
    packed = jnp.broadcast_to(packed[:, None], (32, 2, 24, LANES)).reshape(64, 24, LANES)
    got = lax.all_to_all(packed, ("chip", "core"), split_axis=0, concat_axis=0, tiled=True)

    halves = out_weight.reshape(HEADS, 2, 32, 2, 256)
    mine = lax.dynamic_index_in_dim(halves, core, axis=3, keepdims=False).reshape(64, HALF)
    theirs = lax.dynamic_index_in_dim(halves, 1 - core, axis=3, keepdims=False).reshape(64, HALF)
    arrived = lax.ppermute(theirs, "core", [(0, 1), (1, 0)])
    weight = jnp.concatenate(
        [jnp.where(core == 0, mine, arrived), jnp.where(core == 0, arrived, mine)]
    )

    terms = merge_project(got.reshape(32, 48, LANES), weight)
    terms = lax.all_to_all(
        terms.reshape(128, 8, LANES), ("chip", "tp"), split_axis=0, concat_axis=0, tiled=True
    )
    return final_sum(terms.reshape(64, 16, LANES))


def solution(mesh):
    parts = Mesh(mesh.devices.reshape(32, 2, 4), ("chip", "core", "tp"))
    placed = (
        P(None, "tp", None),
        P(None, ("chip", "core"), "tp", None),
        P(None, ("chip", "core"), "tp", None),
        P(),
        P("tp", ("chip", "core"), None),
    )
    return jax.shard_map(
        local,
        mesh=parts,
        in_specs=placed,
        out_specs=P(None, ("chip", "core", "tp")),
        check_vma=False,
    )
```

time: 1370 us -> 80.7 us (0.06)
  waiting for transfers between devices: 1270 us -> 13.6 us
  blocking collectives: 51.1 us -> 21.8 us
  local copies, waits for them, and re-layouts: 3.29 us -> 22.2 us
    unnamed x2 -> x0, waiting for transfers between devices: 1270 us -> none
    all_gather x1 -> x0, blocking collectives: 51.1 us -> none  [local(): lse_rows = lax.all_gather(block_lse[None], 'kv', axis=0, tiled=True)]
    all_to_all x0 -> x1, blocking collectives: none -> 21.8 us  [local(): lax.all_to_all(terms.reshape(128, 8, LANES), ('chip', 'tp'), split_axis=0...]
    dynamic_slice x0 -> x1, local copies, waits for them, and re-layouts: none -> 14 us  [local(): lax.dynamic_index_in_dim(halves, core, axis=3, keepdims=False)]
  transfers between devices with their start and end apart: 2 -> 2, of which waited for: 1 -> 1; matrix products, arithmetic and copies ran while one was open for 0% -> 12% of each run, Pallas kernels for 0% -> 0%
where the time goes in v1:
time: 80.7 us; the launch traced here: 80 us
  local copies, waits for them, and re-layouts  22.2 us (28%)
  blocking collectives  21.8 us (27%)
  waiting for transfers between devices  13.6 us (17%)
  starting transfers between devices  13.3 us (16%)
  matrix products  6.42 us (8%)
  Pallas kernels  1.68 us (2%)
  other arithmetic  0.87 us (1%)
    all_to_all x1, blocking collectives, local(): lax.all_to_all(terms.reshape(128, 8, LANES), ('chip', 'tp'), split_axis=0...  21.8 us
    dynamic_slice x1, local copies, waits for them, and re-layouts, local(): lax.dynamic_index_in_dim(halves, core, axis=3, keepdims=False)  14 us
    all_to_all x1, waiting for transfers between devices, local(): lax.all_to_all(packed, ('chip', 'core'), split_axis=0, concat_axis=0, til...  13.6 us
    all_to_all x1, starting transfers between devices, local(): lax.all_to_all(packed, ('chip', 'core'), split_axis=0, concat_axis=0, til...  10 us
    unnamed x10, local copies, waits for them, and re-layouts  3.49 us
    dot_general x1, matrix products, attend(): jnp.einsum('bgqd,bpgd->bgqp', grouped, key_cache, preferred_element_type=...  3.48 us
    reshape x1, local copies, waits for them, and re-layouts, local(): halves = out_weight.reshape(HEADS, 2, 32, 2, 256)  3.36 us
    ppermute x1, starting transfers between devices, local(): arrived = lax.ppermute(theirs, 'core', [(0, 1), (1, 0)])  3.24 us
  transfers between devices with their start and end apart: 2, of which 1 were waited for; matrix products, arithmetic and copies ran while one was open for 12% of the time, Pallas kernels for 0%

profile of v1, /device:TPU:1, one launch (start us, length us, event | category | flops | bytes accessed | tf_op | source)
XLA Modules:
  0.0 80.0 jit_solution(3209440971422877059)
XLA Ops:
  0.0 0.0 copy-start
  0.0 3.4 %reshape.111 = bf16[32,2,32,2,256]{4,3,2,1,0:T(2,128)(2,1)S(1)} reshape(bf16[32,2,16384]{2,1,0:T(2,128)(2,1)} %param.11) | data formatting | bytes 4194304 | tf_op jit(solution)/shard_map/reshape | solution.py:143
  3.4 0.0 copy-start.3
  3.4 14.0 %dynamic-slice_reduce_fusion.1 = (bf16[32,2,32,256]{3,2,1,0:T(8,128)(2,1)S(1)}, bf16[32,2,32,256]{3,2,1,0:T(8,128)(2,1)}) fusion(bf16[32,2,32,2,256]{4,3,2,1,0:T(2,128)(2,1)S(1)} %reshape.111, s32[]{:T(128)S(6)} %select_n.58, s32[]{:T(128)S(6)} %select_n.59), kind=kLoop, calls=%fused_computation.6 | loop fusion | bytes 4194312 | tf_op jit(solution)/shard_map/jit(dynamic_index_in_dim)/dynamic_slice | solution.py:144
  17.4 2.8 %copy.20 = bf16[8,8,32,256]{3,1,2,0:T(8,128)(2,1)} copy(bf16[8,8,32,256]{3,2,1,0:T(8,128)(2,1)} %bitcast.20) | data formatting | bytes 2097152
  20.2 3.2 %collective-permute-start = (bf16[64,8192]{1,0:T(8,128)(2,1)}, bf16[64,8192]{1,0:T(8,128)(2,1)S(1)}, u32[]{:S(2)}, u32[]{:S(2)}) collective-permute-start(bf16[64,8192]{1,0:T(8,128)(2,1)} %bitcast.12), channel_id=1, source_target_pairs={{0,4},{4,0},{1,5},{5,1},{2,6},{6,2},{3,7},{7,3},{8,12},{12,8},{9,1... | collective-permute-start | bytes 3145736 | tf_op jit(solution)/shard_map/ppermute | solution.py:146
  23.5 0.0 copy-done.3
  23.5 0.1 broadcast_compare_fusion
  23.5 0.0 copy-done
  23.5 3.5 %select_reduce_fusion = (f32[16,2,16]{2,1,0:T(2,128)S(1)}, f32[16,2,16,512]{3,2,1,0:T(8,128)S(1)}) fusion(pred[16,512]{1,0:T(8,128)(4,1)S(1)} %broadcast_compare_fusion, bf16[16,2,16,128]{3,2,1,0:T(8,128)(2,1)S(1)} %bitcast.14, bf16[16,512,2,128]{3,2,1,0:T(2,128)(2,1)} %param.8), kind=kOutput, calls=%fused_computation.11 | convolution fusion | flops 67894784 | bytes 5384192 | tf_op jit(solution)/shard_map/bgqd,bpgd->bgqp/dot_general | solution.py:112
  27.0 0.1 reduce_max.12
  27.1 0.4 fusion.13
  27.5 0.1 reduce-precision_divide_fusion
  27.6 2.9 %fusion.10 = bf16[16,2,16,128]{3,2,1,0:T(8,128)(2,1)S(1)} fusion(bf16[16,512,2,128]{3,2,1,0:T(2,128)(2,1)} %param.9, f32[16,2,16,512]{3,2,1,0:T(8,128)S(1)} %get-tuple-element.15, f32[16,2,16]{2,1,0:T(2,128)S(1)} %get-tuple-element.14, pred[16,512]{1,0:T(8,128)(4,1)S(1)} %broadcast_compare_fusion, f32[16,2,16]{2,1,0:T(2,128)S(1)} %get-tuple-element.7), kind=kOutput, calls=%fused_computation.9 | convolution fusion | flops 68026368 | bytes 5386240 | tf_op jit(solution)/shard_map/bgqp,bpgd->bgqd/dot_general | solution.py:118
  30.5 0.1 copy.14
  30.6 0.1 reshape.108
  30.7 0.1 max.21
  30.8 0.1 gt.20
  31.0 0.8 %broadcast_in_dim.42 = bf16[32,2,24,128]{3,2,1,0:T(8,128)(2,1)} broadcast(bf16[32,24,128]{2,1,0:T(8,128)(2,1)S(1)} %pad_maximum_fusion.1), dimensions={0,2,3} | broadcast | bytes 589824 | tf_op jit(solution)/shard_map/broadcast_in_dim | solution.py:140
  31.8 10.0 %all-to-all-start = ((bf16[64,24,128]{2,1,0:T(8,128)(2,1)}), bf16[64,24,128]{2,1,0:T(8,128)(2,1)S(1)}, u32[]{:S(2)}, u32[]{:S(2)}) async-start(bf16[64,24,128]{2,1,0:T(8,128)(2,1)} %bitcast.3), calls=%async_computation | async-start | bytes 786432 | tf_op jit(solution)/shard_map/all_to_all | solution.py:141
  41.9 0.6 copy.19
  42.5 0.0 collective-permute-done
  42.5 0.0 copy-start.1
  42.5 0.0 copy-start.2
  42.5 0.1 broadcast_select_fusion.1
  42.7 0.2 pad_maximum_fusion.weight_ref
  42.9 13.6 %all-to-all-done = bf16[64,24,128]{2,1,0:T(8,128)(2,1)S(1)} async-done(((bf16[64,24,128]{2,1,0:T(8,128)(2,1)}), bf16[64,24,128]{2,1,0:T(8,128)(2,1)S(1)}, u32[]{:S(2)}, u32[]{:S(2)}) %all-to-all-start) | async-done | bytes 393248 | tf_op jit(solution)/shard_map/all_to_all | solution.py:141
  56.5 0.0 copy-done.1
  56.5 0.0 copy-done.2
  56.5 1.0 %shard_map.73 = bf16[64,16,128]{2,1,0:T(8,128)(2,1)S(1)} custom-call(bf16[32,48,128]{2,1,0:T(8,128)(2,1)S(1)} %bitcast.15, bf16[128,8192]{1,0:T(8,128)(2,1)S(1)} %pad_maximum_fusion.weight_ref, bf16[512,128]{1,0:T(8,128)(2,1)S(1)} %copy-done.1, bf16[64,16]{1,0:T(8,128)(2,1)S(1)} %copy-done.2), custom_call_target="tpu_custom_call" | custom-call | flops 34000000 | bytes 3000000 | tf_op jit(solution)/shard_map/pallas_call | solution.py:71
  57.4 21.8 %all_to_all.10 = bf16[128,8,128]{2,1,0:T(8,128)(2,1)S(1)} all-to-all(bf16[128,8,128]{2,1,0:T(8,128)(2,1)S(1)} %bitcast.17), channel_id=1, replica_groups=mesh['chip'=32,'core'=2,'tp'=4] {'chip','tp'}, dimensions={0} | all-to-all | bytes 524288 | tf_op jit(solution)/shard_map/all_to_all | solution.py:152
  79.3 0.7 shard_map.74
  (5 shorter events, 0.1 us)
Async XLA Ops:
  0.0 23.5 %copy-start = (bf16[16,32,128]{2,1,0:T(8,128)(2,1)S(1)}, bf16[16,32,128]{2,1,0:T(8,128)(2,1)}, u32[]{:S(2)}) copy-start(bf16[16,32,128]{2,1,0:T(8,128)(2,1)} %param.7) | copy-start | bytes 393220
  3.4 20.1 %copy-start.3 = (s32[16]{0:T(128)S(1)}, s32[16]{0:T(128)}, u32[]{:S(2)}) copy-start(s32[16]{0:T(128)} %param.10) | copy-start | bytes 196
  20.2 22.3 %collective-permute-start = (bf16[64,8192]{1,0:T(8,128)(2,1)}, bf16[64,8192]{1,0:T(8,128)(2,1)S(1)}, u32[]{:S(2)}, u32[]{:S(2)}) collective-permute-start(bf16[64,8192]{1,0:T(8,128)(2,1)} %bitcast.12), channel_id=1, source_target_pairs={{0,4},{4,0},{1,5},{5,1},{2,6},{6,2},{3,7},{7,3},{8,12},{12,8},{9,1... | collective-permute-start | bytes 3145736 | tf_op jit(solution)/shard_map/ppermute | solution.py:146
  31.8 24.6 %all-to-all-start = ((bf16[64,24,128]{2,1,0:T(8,128)(2,1)}), bf16[64,24,128]{2,1,0:T(8,128)(2,1)S(1)}, u32[]{:S(2)}, u32[]{:S(2)}) async-start(bf16[64,24,128]{2,1,0:T(8,128)(2,1)} %bitcast.3), calls=%async_computation | async-start | bytes 786432 | tf_op jit(solution)/shard_map/all_to_all | solution.py:141
  42.5 14.0 %copy-start.1 = (bf16[512,128]{1,0:T(8,128)(2,1)S(1)}, bf16[512,128]{1,0:T(8,128)(2,1)}, u32[]{:S(2)}) copy-start(bf16[512,128]{1,0:T(8,128)(2,1)} %constant.43.clone.spread_ref) | copy-start | bytes 393220
  42.5 14.0 %copy-start.2 = (bf16[64,16]{1,0:T(8,128)(2,1)S(1)}, bf16[64,16]{1,0:T(8,128)(2,1)}, u32[]{:S(2)}) copy-start(bf16[64,16]{1,0:T(8,128)(2,1)} %constant.44.clone.repeat_ref) | copy-start | bytes 6148

commit v2 on v1

--- a/solution.py
+++ b/solution.py
@@ -14,6 +14,8 @@
 LANES = 128
 CHIP_FEATURES = 4
 HALF = 8192
+PER = 4
+GROUPS = SEQS // PER
 
 
 def spread_table():
@@ -101,52 +103,152 @@
     )(got)
 
 
-def attend(query, key_cache, value_cache, lengths, block_index):
-    batch, local_heads, head_size = query.shape
-    positions_dev = key_cache.shape[1]
-    local_kv = key_cache.shape[2]
-    group = local_heads // local_kv
-    positions = block_index * positions_dev + jnp.arange(positions_dev, dtype=jnp.int32)
-    live = (positions[None, :] < lengths[:, None])[:, None, None, :]
-    grouped = query.reshape(batch, local_kv, group, head_size)
-    scores = jnp.einsum("bgqd,bpgd->bgqp", grouped, key_cache, preferred_element_type=jnp.float32)
-    scores = scores * jnp.float32(head_size**-0.5)
-    masked = jnp.where(live, scores, jnp.float32(-1e30))
-    block_max = jnp.max(masked, axis=-1)
-    weights = jnp.where(live, jnp.exp(scores - block_max[..., None]), jnp.float32(0.0))
-    block_total = jnp.sum(weights, axis=-1)
-    summed = jnp.einsum(
-        "bgqp,bpgd->bgqd",
-        weights.astype(jnp.bfloat16),
-        value_cache,
-        preferred_element_type=jnp.float32,
-    )
-    floored = jnp.maximum(block_total, jnp.float32(1.0))
-    coarse = lax.reduce_precision(block_max + jnp.log(floored), 8, 7)
-    some = block_total > 0
-    fine = jnp.where(some, floored * jnp.exp(jnp.where(some, block_max - coarse, 0.0)), 0.0)
-    fine = lax.reduce_precision(fine, 8, 7)
-    scaled = (summed * (fine / floored)[..., None]).astype(jnp.bfloat16)
-    features = scaled.reshape(batch * local_heads, head_size).T.reshape(32, 16, LANES)
-    stats = jnp.concatenate([coarse.reshape(4, LANES), fine.reshape(4, LANES)]).astype(jnp.bfloat16)
-    stats = jnp.broadcast_to(stats[None], (32, 8, LANES))
-    return jnp.concatenate([features, stats], axis=1)
+def attend_kernel(
+    lengths_hbm,
+    query_hbm,
+    key_hbm,
+    value_hbm,
+    out_ref,
+    lengths_ref,
+    query_ref,
+    keys,
+    values,
+    outs,
+    turned,
+    small_sem,
+    key_sem,
+    value_sem,
+):
+    width = key_hbm.shape[1]
+    block_index = lax.axis_index("chip") * 2 + lax.axis_index("core")
+    base = block_index * (width // 2)
+    query_copy = pltpu.make_async_copy(query_hbm, query_ref, small_sem.at[0])
+    lengths_copy = pltpu.make_async_copy(lengths_hbm, lengths_ref, small_sem.at[1])
+    key_copies = []
+    value_copies = []
+    for b in range(SEQS):
+        key_copies.append(pltpu.make_async_copy(key_hbm.at[b], keys.at[b], key_sem.at[b]))
+        value_copies.append(pltpu.make_async_copy(value_hbm.at[b], values.at[b], value_sem.at[b]))
+    query_copy.start()
+    lengths_copy.start()
+    for t in range(GROUPS + 1):
+        if t < GROUPS:
+            for b in range(PER * t, PER * t + PER):
+                key_copies[b].start()
+        if t > 0:
+            for b in range(PER * t - PER, PER * t):
+                value_copies[b].start()
+
+    column = lax.broadcasted_iota(jnp.int32, (HEADS, width), 1)
+    row = lax.broadcasted_iota(jnp.int32, (HEADS, width), 0)
+    position = jnp.where((column % 2) == (row // 16), column // 2, jnp.int32(1 << 30))
+    lane = lax.broadcasted_iota(jnp.int32, (HEADS, LANES), 1)
+    factor = jnp.float32(LANES**-0.5)
+    query_copy.wait()
+    lengths_copy.wait()
+    scores, weights, tops, totals, stats = {}, {}, {}, {}, [0.0] * 4
+    for t in range(GROUPS + 2):
+        first = range(PER * t, PER * t + PER) if t < GROUPS else ()
+        second = range(PER * (t - 1), PER * t) if 1 <= t <= GROUPS else ()
+        third = range(PER * (t - 2), PER * (t - 1)) if t >= 2 else ()
+        for b in first:
+            key_copies[b].wait()
+        for b in third:
+            value_copies[b].wait()
+        for b in first:
+            raw = lax.dot_general(
+                query_ref[b],
+                keys[b],
+                (((1,), (1,)), ((), ())),
+                preferred_element_type=jnp.float32,
+            )
+            scores[b] = jnp.where(position < lengths_ref[b] - base, raw, jnp.float32(-1e30))
+        for b in second:
+            top = jnp.max(scores[b], axis=1, keepdims=True)
+            weight = jnp.exp((scores[b] - top) * factor)
+            totals[b] = jnp.sum(weight, axis=1, keepdims=True)
+            tops[b] = top * factor
+            weights[b] = weight.astype(jnp.bfloat16)
+        for b in third:
+            summed = jnp.dot(weights[b], values[b], preferred_element_type=jnp.float32)
+            coarse = (tops[b] + jnp.log(totals[b])).astype(jnp.bfloat16).astype(jnp.float32)
+            fine = totals[b] * jnp.exp(tops[b] - coarse)
+            fine = fine.astype(jnp.bfloat16).astype(jnp.float32)
+            fine = jnp.where(lengths_ref[b] > base, fine, 0.0)
+            outs[b * HEADS : b * HEADS + HEADS] = summed * (fine / totals[b])
+            k = b // 4
+            stats[b % 4] = jnp.where(
+                lane == k, coarse, jnp.where(lane == k + 4, fine, stats[b % 4])
+            )
+            if b % 4 == 3:
+                turned[pl.ds(k, LANES, stride=4), :] = outs[k * LANES : k * LANES + LANES].T
+    packed = jnp.concatenate(stats, axis=0).T[0:8]
+    features = turned[...].reshape(32, 16, LANES)
+    packed = jnp.broadcast_to(packed[None], (32, 8, LANES))
+    out_ref[...] = jnp.concatenate([features, packed, features, packed], axis=1).astype(
+        jnp.bfloat16
+    )
+
+
+def attend(query, key_cache, value_cache, lengths):
+    width = key_cache.shape[1] * key_cache.shape[2]
+    keys = key_cache.reshape(SEQS, width, LANES)
+    values = value_cache.reshape(SEQS, width, LANES)
+    vmem = pl.BlockSpec(memory_space=pltpu.VMEM)
+    hbm = pl.BlockSpec(memory_space=pltpu.HBM)
+    return pl.pallas_call(
+        attend_kernel,
+        out_shape=jax.ShapeDtypeStruct((32, 48, LANES), jnp.bfloat16),
+        in_specs=[hbm] * 4,
+        out_specs=vmem,
+        scratch_shapes=[
+            pltpu.SMEM((SEQS,), jnp.int32),
+            pltpu.VMEM((SEQS, HEADS, LANES), jnp.bfloat16),
+            pltpu.VMEM((SEQS, width, LANES), jnp.bfloat16),
+            pltpu.VMEM((SEQS, width, LANES), jnp.bfloat16),
+            pltpu.VMEM((512, LANES), jnp.float32),
+            pltpu.VMEM((512, LANES), jnp.float32),
+            pltpu.SemaphoreType.DMA((2,)),
+            pltpu.SemaphoreType.DMA((SEQS,)),
+            pltpu.SemaphoreType.DMA((SEQS,)),
+        ],
+        compiler_params=pltpu.CompilerParams(vmem_limit_bytes=60 * 1024 * 1024),
+        cost_estimate=pl.CostEstimate(
+            flops=270_000_000, bytes_accessed=8_800_000, transcendentals=540_000
+        ),
+    )(lengths, query, keys, values)
+
+
+def split_kernel(own_ref, other_ref, out_ref):
+    core = lax.axis_index("core")
+    for t in range(own_ref.shape[2] // 512):
+        start = pl.multiple_of(t * 512 + core * 256, 256)
+        for which, ref in ((core, own_ref), (1 - core, other_ref)):
+            rows = pl.ds(pl.multiple_of(which * 64, 64), 64)
+            piece = ref[:, :, pl.ds(start, 256)]
+            out_ref[rows, t * 256 : (t + 1) * 256] = piece.reshape(64, 256)
+
+
+def split_weight(own, other):
+    vmem = pl.BlockSpec(memory_space=pltpu.VMEM)
+    return pl.pallas_call(
+        split_kernel,
+        out_shape=jax.ShapeDtypeStruct((LANES, HALF), jnp.bfloat16),
+        in_specs=[vmem, vmem],
+        out_specs=vmem,
+        compiler_params=pltpu.CompilerParams(vmem_limit_bytes=16 * 1024 * 1024),
+        cost_estimate=pl.CostEstimate(flops=0, bytes_accessed=4_194_304, transcendentals=0),
+    )(own, other)
 
 
 def local(query, key_cache, value_cache, lengths, out_weight):
-    core = lax.axis_index("core")
-    block_index = lax.axis_index("chip") * 2 + core
-    packed = attend(query, key_cache, value_cache, lengths, block_index)
-    packed = jnp.broadcast_to(packed[:, None], (32, 2, 24, LANES)).reshape(64, 24, LANES)
-    got = lax.all_to_all(packed, ("chip", "core"), split_axis=0, concat_axis=0, tiled=True)
-
-    halves = out_weight.reshape(HEADS, 2, 32, 2, 256)
-    mine = lax.dynamic_index_in_dim(halves, core, axis=3, keepdims=False).reshape(64, HALF)
-    theirs = lax.dynamic_index_in_dim(halves, 1 - core, axis=3, keepdims=False).reshape(64, HALF)
-    arrived = lax.ppermute(theirs, "core", [(0, 1), (1, 0)])
-    weight = jnp.concatenate(
-        [jnp.where(core == 0, mine, arrived), jnp.where(core == 0, arrived, mine)]
-    )
+    packed = attend(query, key_cache, value_cache, lengths)
+    packed, out_weight = lax.optimization_barrier((packed, out_weight))
+    got = lax.all_to_all(
+        packed.reshape(64, 24, LANES), ("chip", "core"), split_axis=0, concat_axis=0, tiled=True
+    )
+    other = lax.ppermute(out_weight, "core", [(0, 1), (1, 0)])
+    weight = split_weight(out_weight, other)
 
     terms = merge_project(got.reshape(32, 48, LANES), weight)
     terms = lax.all_to_all(

time: 80.7 us -> 59.6 us (0.74)
  local copies, waits for them, and re-layouts: 22.2 us -> 1.6 us
  Pallas kernels: 1.68 us -> 11.9 us
  matrix products: 6.42 us -> 0 us
  waiting for transfers between devices: 13.6 us -> 10.3 us
  other arithmetic: 0.87 us -> 0 us
    dynamic_slice x1 -> x0, local copies, waits for them, and re-layouts: 14 us -> none  [local(): lax.dynamic_index_in_dim(halves, core, axis=3, keepdims=False)]
    pallas_call x0 -> x2, Pallas kernels: none -> 10.2 us  [the longest x1 7.46 us: attend(): pl.pallas_call(attend_kernel, out_shape=jax.ShapeDtypeStruct((32, 48, LAN...]
    dot_general x2 -> x0, matrix products: 6.42 us -> none  [the longest x1 3.48 us: attend(): jnp.einsum('bgqd,bpgd->bgqp', grouped, key_cache, preferred_element_type=...]
    reshape x3 -> x0, local copies, waits for them, and re-layouts: 3.57 us -> none  [the longest x1 3.36 us: local(): halves = out_weight.reshape(HEADS, 2, 32, 2, 256)]
    all_to_all x1, waiting for transfers between devices: 13.6 us -> 10.3 us  [local(): lax.all_to_all(packed.reshape(64, 24, LANES), ('chip', 'core'), split_axi...]
    unnamed x10 -> x8, local copies, waits for them, and re-layouts: 3.49 us -> 1.6 us
    broadcast_in_dim x2 -> x0, local copies, waits for them, and re-layouts: 0.82 us -> none  [the longest x1 0.81 us: local(): jnp.broadcast_to(packed[:, None], (32, 2, 24, LANES)).reshape(64, 24, LANES)]
  transfers between devices with their start and end apart: 2 -> 2, of which waited for: 1 -> 1; matrix products, arithmetic and copies ran while one was open for 12% -> 0% of each run, Pallas kernels for 0% -> 5%
where the time goes in v2:
time: 59.6 us; the launch traced here: 59 us
  blocking collectives  21.8 us (37%)
  starting transfers between devices  13.4 us (22%)
  Pallas kernels  11.9 us (20%)
  waiting for transfers between devices  10.3 us (17%)
  local copies, waits for them, and re-layouts  1.6 us (3%)
    all_to_all x1, blocking collectives, local(): lax.all_to_all(terms.reshape(128, 8, LANES), ('chip', 'tp'), split_axis=0...  21.8 us
    all_to_all x1, waiting for transfers between devices, local(): lax.all_to_all(packed.reshape(64, 24, LANES), ('chip', 'core'), split_axi...  10.3 us
    all_to_all x1, starting transfers between devices, local(): lax.all_to_all(packed.reshape(64, 24, LANES), ('chip', 'core'), split_axi...  10 us
    pallas_call x1, Pallas kernels, attend(): pl.pallas_call(attend_kernel, out_shape=jax.ShapeDtypeStruct((32, 48, LAN...  7.46 us
    ppermute x1, starting transfers between devices, local(): other = lax.ppermute(out_weight, 'core', [(0, 1), (1, 0)])  3.32 us
    pallas_call x1, Pallas kernels, split_weight(): pl.pallas_call(split_kernel, out_shape=jax.ShapeDtypeStruct((LANES, HALF)...  2.71 us
    unnamed x8, local copies, waits for them, and re-layouts  1.6 us
  transfers between devices with their start and end apart: 2, of which 1 were waited for; matrix products, arithmetic and copies ran while one was open for 0% of the time, Pallas kernels for 5%

profile of v2, /device:TPU:1, one launch (start us, length us, event | category | flops | bytes accessed | tf_op | source)
XLA Modules:
  0.0 59.0 jit_solution(10089945051445689883)
XLA Ops:
  0.0 0.0 copy-start
  0.0 7.5 %shard_map.73 = bf16[32,48,128]{2,1,0:T(8,128)(2,1)} custom-call(s32[16]{0:T(128)} %lengths_hbm.1, bf16[16,32,128]{2,1,0:T(8,128)(2,1)} %query_hbm.1, bf16[16,1024,128]{2,1,0:T(8,128)(2,1)} %bitcast.9, bf16[16,1024,128]{2,1,0:T(8,128)(2,1)} %bitcast.10), custom_call_target="tpu_custom_call" | custom-call | flops 270000000 | bytes 8800000 | tf_op jit(solution)/shard_map/pallas_call | solution.py:199
  7.5 0.0 copy-done
  7.5 3.3 %collective-permute-start = (bf16[32,2,16384]{2,1,0:T(2,128)(2,1)S(1)}, bf16[32,2,16384]{2,1,0:T(2,128)(2,1)}, u32[]{:S(2)}, u32[]{:S(2)}) collective-permute-start(bf16[32,2,16384]{2,1,0:T(2,128)(2,1)S(1)} %copy-done), channel_id=1, source_target_pairs={{0,4},{4,0},{1,5},{5,1},{2,6},{6,2},{3,7},{7,3},{8,12},{12,8},{9,1... | collective-permute-start | bytes 6291464 | tf_op jit(solution)/shard_map/ppermute | solution.py:250
  10.8 10.0 %all-to-all-start = ((bf16[64,24,128]{2,1,0:T(8,128)(2,1)}), bf16[64,24,128]{2,1,0:T(8,128)(2,1)S(1)}, u32[]{:S(2)}, u32[]{:S(2)}) async-start(bf16[64,24,128]{2,1,0:T(8,128)(2,1)} %bitcast.11), calls=%async_computation | async-start | bytes 786432 | tf_op jit(solution)/shard_map/all_to_all | solution.py:247
  20.8 0.0 collective-permute-done.other_ref
  20.9 0.0 copy-start.1
  20.9 1.6 %copy-done.1 = bf16[32,2,16384]{2,1,0:T(2,128)(2,1)S(1)} copy-done((bf16[32,2,16384]{2,1,0:T(2,128)(2,1)S(1)}, bf16[32,2,16384]{2,1,0:T(2,128)(2,1)}, u32[]{:S(2)}) %copy-start.1) | copy-done | bytes 2097176
  22.4 0.0 copy-start.2
  22.5 0.0 copy-start.3
  22.5 2.7 %shard_map.74.weight_ref = bf16[128,8192]{1,0:T(8,128)(2,1)S(1)} custom-call(bf16[32,2,16384]{2,1,0:T(2,128)(2,1)S(1)} %copy-done.1, bf16[32,2,16384]{2,1,0:T(2,128)(2,1)} %collective-permute-done.other_ref), custom_call_target="tpu_custom_call" | custom-call | bytes 4194304 | tf_op jit(solution)/shard_map/pallas_call | solution.py:234
  25.2 10.3 %all-to-all-done = bf16[64,24,128]{2,1,0:T(8,128)(2,1)S(1)} async-done(((bf16[64,24,128]{2,1,0:T(8,128)(2,1)}), bf16[64,24,128]{2,1,0:T(8,128)(2,1)S(1)}, u32[]{:S(2)}, u32[]{:S(2)}) %all-to-all-start) | async-done | bytes 393248 | tf_op jit(solution)/shard_map/all_to_all | solution.py:247
  35.5 0.0 copy-done.2
  35.5 0.0 copy-done.3
  35.5 1.0 %shard_map.75 = bf16[64,16,128]{2,1,0:T(8,128)(2,1)S(1)} custom-call(bf16[32,48,128]{2,1,0:T(8,128)(2,1)S(1)} %bitcast.6, bf16[128,8192]{1,0:T(8,128)(2,1)S(1)} %shard_map.74.weight_ref, bf16[512,128]{1,0:T(8,128)(2,1)S(1)} %copy-done.2, bf16[64,16]{1,0:T(8,128)(2,1)S(1)} %copy-done.3), custom_call_target="tpu_custom_call" | custom-call | flops 34000000 | bytes 3000000 | tf_op jit(solution)/shard_map/pallas_call | solution.py:73
  36.4 21.8 %all_to_all.10 = bf16[128,8,128]{2,1,0:T(8,128)(2,1)S(1)} all-to-all(bf16[128,8,128]{2,1,0:T(8,128)(2,1)S(1)} %bitcast.8), channel_id=1, replica_groups=mesh['chip'=32,'core'=2,'tp'=4] {'chip','tp'}, dimensions={0} | all-to-all | bytes 524288 | tf_op jit(solution)/shard_map/all_to_all | solution.py:254
  58.2 0.7 %shard_map.76 = bf16[16,64]{1,0:T(8,128)(2,1)} custom-call(bf16[64,16,128]{2,1,0:T(8,128)(2,1)S(1)} %bitcast.7), custom_call_target="tpu_custom_call" | custom-call | flops 131072 | bytes 264192 | tf_op jit(solution)/shard_map/pallas_call | solution.py:96
Async XLA Ops:
  0.0 7.5 %copy-start = (bf16[32,2,16384]{2,1,0:T(2,128)(2,1)S(1)}, bf16[32,2,16384]{2,1,0:T(2,128)(2,1)}, u32[]{:S(2)}) copy-start(bf16[32,2,16384]{2,1,0:T(2,128)(2,1)} %own_ref) | copy-start | bytes 6291460
  7.5 13.4 %collective-permute-start = (bf16[32,2,16384]{2,1,0:T(2,128)(2,1)S(1)}, bf16[32,2,16384]{2,1,0:T(2,128)(2,1)}, u32[]{:S(2)}, u32[]{:S(2)}) collective-permute-start(bf16[32,2,16384]{2,1,0:T(2,128)(2,1)S(1)} %copy-done), channel_id=1, source_target_pairs={{0,4},{4,0},{1,5},{5,1},{2,6},{6,2},{3,7},{7,3},{8,12},{12,8},{9,1... | collective-permute-start | bytes 6291464 | tf_op jit(solution)/shard_map/ppermute | solution.py:250
  10.8 24.6 %all-to-all-start = ((bf16[64,24,128]{2,1,0:T(8,128)(2,1)}), bf16[64,24,128]{2,1,0:T(8,128)(2,1)S(1)}, u32[]{:S(2)}, u32[]{:S(2)}) async-start(bf16[64,24,128]{2,1,0:T(8,128)(2,1)} %bitcast.11), calls=%async_computation | async-start | bytes 786432 | tf_op jit(solution)/shard_map/all_to_all | solution.py:247
  20.9 1.6 %copy-start.1 = (bf16[32,2,16384]{2,1,0:T(2,128)(2,1)S(1)}, bf16[32,2,16384]{2,1,0:T(2,128)(2,1)}, u32[]{:S(2)}) copy-start(bf16[32,2,16384]{2,1,0:T(2,128)(2,1)} %own_ref) | copy-start | bytes 6291460
  22.4 13.0 %copy-start.2 = (bf16[512,128]{1,0:T(8,128)(2,1)S(1)}, bf16[512,128]{1,0:T(8,128)(2,1)}, u32[]{:S(2)}) copy-start(bf16[512,128]{1,0:T(8,128)(2,1)} %constant.4.clone.spread_ref) | copy-start | bytes 393220
  22.5 13.0 %copy-start.3 = (bf16[64,16]{1,0:T(8,128)(2,1)S(1)}, bf16[64,16]{1,0:T(8,128)(2,1)}, u32[]{:S(2)}) copy-start(bf16[64,16]{1,0:T(8,128)(2,1)} %constant.5.clone.repeat_ref) | copy-start | bytes 6148

commit v3 on v2

--- a/solution.py
+++ b/solution.py
@@ -15,6 +15,7 @@
 CHIP_FEATURES = 4
 HALF = 8192
 PER = 4
+AHEAD = 4
 GROUPS = SEQS // PER
 
 
@@ -34,17 +35,40 @@
     return table.reshape(64, 16)
 
 
-def merge_project_kernel(got_ref, weight_ref, spread_ref, repeat_ref, out_ref):
-    got = got_ref[...].astype(jnp.float32).reshape(64, 24, LANES)
+def merge_kernel(got_ref, out_ref):
+    got = got_ref[...].astype(jnp.float32).reshape(32, 24, LANES)
     stats = got[:, 16:24]
     swapped = pltpu.roll(stats, 4, 1)
     upper = lax.broadcasted_iota(jnp.int32, stats.shape, 1) < 4
     coarse = jnp.where(upper, stats, swapped)
     fine = jnp.where(upper, swapped, stats)
-    scale = jnp.exp(coarse - jnp.max(coarse, axis=0, keepdims=True))
-    total = jnp.sum(scale * fine, axis=0)
-    first = jnp.sum(scale * got[:, 0:8], axis=0) / total
-    second = jnp.sum(scale * got[:, 8:16], axis=0) / total
+    highest = jnp.max(coarse, axis=0)
+    scale = jnp.exp(coarse - highest[None])
+    out_ref[0:8] = jnp.sum(scale * got[:, 0:8], axis=0)
+    out_ref[8:16] = jnp.sum(scale * got[:, 8:16], axis=0)
+    out_ref[16:24] = highest
+    out_ref[24:32] = jnp.sum(scale * fine, axis=0)
+
+
+def merge(got):
+    vmem = pl.BlockSpec(memory_space=pltpu.VMEM)
+    return pl.pallas_call(
+        merge_kernel,
+        out_shape=jax.ShapeDtypeStruct((32, LANES), jnp.float32),
+        in_specs=[vmem],
+        out_specs=vmem,
+        compiler_params=pltpu.CompilerParams(vmem_limit_bytes=16 * 1024 * 1024),
+        cost_estimate=pl.CostEstimate(flops=400_000, bytes_accessed=212_992, transcendentals=32768),
+    )(got)
+
+
+def project_kernel(own_ref, other_ref, weight_ref, spread_ref, repeat_ref, out_ref):
+    highest = jnp.maximum(own_ref[16:24], other_ref[16:24])
+    own_scale = jnp.exp(own_ref[16:24] - highest)
+    other_scale = jnp.exp(other_ref[16:24] - highest)
+    total = own_scale * own_ref[24:32] + other_scale * other_ref[24:32]
+    first = (own_scale * own_ref[0:8] + other_scale * other_ref[0:8]) / total
+    second = (own_scale * own_ref[8:16] + other_scale * other_ref[8:16]) / total
     merged = jnp.concatenate([first, second], axis=0).astype(jnp.bfloat16)
     rows = jnp.dot(repeat_ref[...], merged, preferred_element_type=jnp.float32)
     lane_group = lax.broadcasted_iota(jnp.int32, rows.shape, 1) // 32
@@ -68,17 +92,18 @@
             )
 
 
-def merge_project(got, weight):
-    vmem = pl.BlockSpec(memory_space=pltpu.VMEM)
-    return pl.pallas_call(
-        merge_project_kernel,
+def project(own, other, weight):
+    vmem = pl.BlockSpec(memory_space=pltpu.VMEM)
+    return pl.pallas_call(
+        project_kernel,
         out_shape=jax.ShapeDtypeStruct((HALF // LANES, 16, LANES), jnp.bfloat16),
-        in_specs=[vmem] * 4,
+        in_specs=[vmem] * 5,
         out_specs=vmem,
         compiler_params=pltpu.CompilerParams(vmem_limit_bytes=24 * 1024 * 1024),
         cost_estimate=pl.CostEstimate(flops=34_000_000, bytes_accessed=3_000_000, transcendentals=65536),
     )(
-        got,
+        own,
+        other,
         weight,
         jnp.asarray(spread_table(), jnp.bfloat16),
         jnp.asarray(repeat_table(), jnp.bfloat16),
@@ -131,13 +156,15 @@
         value_copies.append(pltpu.make_async_copy(value_hbm.at[b], values.at[b], value_sem.at[b]))
     query_copy.start()
     lengths_copy.start()
+    loads = []
     for t in range(GROUPS + 1):
         if t < GROUPS:
-            for b in range(PER * t, PER * t + PER):
-                key_copies[b].start()
+            loads.append(key_copies[PER * t : PER * t + PER])
         if t > 0:
-            for b in range(PER * t - PER, PER * t):
-                value_copies[b].start()
+            loads.append(value_copies[PER * t - PER : PER * t])
+    for copy in sum(loads[:AHEAD], []):
+        copy.start()
+    begun, used = AHEAD, 0
 
     column = lax.broadcasted_iota(jnp.int32, (HEADS, width), 1)
     row = lax.broadcasted_iota(jnp.int32, (HEADS, width), 0)
@@ -155,6 +182,10 @@
             key_copies[b].wait()
         for b in third:
             value_copies[b].wait()
+        used += (len(first) + len(third)) // PER
+        for copy in sum(loads[begun : used + AHEAD], []):
+            copy.start()
+        begun = max(begun, used + AHEAD)
         for b in first:
             raw = lax.dot_general(
                 query_ref[b],
@@ -183,11 +214,11 @@
             if b % 4 == 3:
                 turned[pl.ds(k, LANES, stride=4), :] = outs[k * LANES : k * LANES + LANES].T
     packed = jnp.concatenate(stats, axis=0).T[0:8]
-    features = turned[...].reshape(32, 16, LANES)
-    packed = jnp.broadcast_to(packed[None], (32, 8, LANES))
-    out_ref[...] = jnp.concatenate([features, packed, features, packed], axis=1).astype(
-        jnp.bfloat16
-    )
+    features = turned[...].reshape(16, 2, 16, LANES)
+    packed = jnp.broadcast_to(packed[None], (16, 8, LANES))
+    out_ref[...] = jnp.concatenate(
+        [features[:, 0], packed, features[:, 1], packed], axis=1
+    ).astype(jnp.bfloat16)
 
 
 def attend(query, key_cache, value_cache, lengths):
@@ -198,7 +229,7 @@
     hbm = pl.BlockSpec(memory_space=pltpu.HBM)
     return pl.pallas_call(
         attend_kernel,
-        out_shape=jax.ShapeDtypeStruct((32, 48, LANES), jnp.bfloat16),
+        out_shape=jax.ShapeDtypeStruct((16, 48, LANES), jnp.bfloat16),
         in_specs=[hbm] * 4,
         out_specs=vmem,
         scratch_shapes=[
@@ -245,12 +276,14 @@
     packed = attend(query, key_cache, value_cache, lengths)
     packed, out_weight = lax.optimization_barrier((packed, out_weight))
     got = lax.all_to_all(
-        packed.reshape(64, 24, LANES), ("chip", "core"), split_axis=0, concat_axis=0, tiled=True
+        packed.reshape(32, 24, LANES), "chip", split_axis=0, concat_axis=0, tiled=True
     )
     other = lax.ppermute(out_weight, "core", [(0, 1), (1, 0)])
     weight = split_weight(out_weight, other)
 
-    terms = merge_project(got.reshape(32, 48, LANES), weight)
+    part = merge(got.reshape(16, 48, LANES))
+    other_part = lax.ppermute(part, "core", [(0, 1), (1, 0)])
+    terms = project(part, other_part, weight)
     terms = lax.all_to_all(
         terms.reshape(128, 8, LANES), ("chip", "tp"), split_axis=0, concat_axis=0, tiled=True
     )

time: 59.6 us -> 55.5 us (0.931)
  blocking collectives: 21.8 us -> 40.2 us
  waiting for transfers between devices: 10.3 us -> 0.01 us
  starting transfers between devices: 13.4 us -> 6.2 us
  Pallas kernels: 11.9 us -> 8.81 us
  local copies, waits for them, and re-layouts: 1.6 us -> 0.02 us
    all_to_all x0 -> x1, blocking collectives: none -> 19.1 us  [local(): lax.all_to_all(packed.reshape(32, 24, LANES), 'chip', split_axis=0, conca...]
    all_to_all x1 -> x0, waiting for transfers between devices: 10.3 us -> none  [local(): lax.all_to_all(packed.reshape(64, 24, LANES), ('chip', 'core'), split_axi...]
    all_to_all x1 -> x0, starting transfers between devices: 10 us -> none  [local(): lax.all_to_all(packed.reshape(64, 24, LANES), ('chip', 'core'), split_axi...]
    ppermute x0 -> x1, starting transfers between devices: none -> 2.87 us  [local(): other_part = lax.ppermute(part, 'core', [(0, 1), (1, 0)])]
    pallas_call x1, Pallas kernels: 2.71 us -> 1.09 us  [split_weight(): pl.pallas_call(split_kernel, out_shape=jax.ShapeDtypeStruct((LANES, HALF)...]
    unnamed x8 -> x6, local copies, waits for them, and re-layouts: 1.6 us -> 0.02 us
    pallas_call x2 -> x3, Pallas kernels: 8.42 us -> 6.99 us  [the longest x1 6.2 us: attend(): pl.pallas_call(attend_kernel, out_shape=jax.ShapeDtypeStruct((16, 48, LAN...]
    all_to_all x1, blocking collectives: 21.8 us -> 21.1 us  [local(): lax.all_to_all(terms.reshape(128, 8, LANES), ('chip', 'tp'), split_axis=0...]
  transfers between devices with their start and end apart: 2 -> 2, of which waited for: 1 -> 0; matrix products, arithmetic and copies ran while one was open for 0% -> 0% of each run, Pallas kernels for 5% -> 2%
where the time goes in v3:
time: 55.5 us; the launch traced here: 55.3 us
  blocking collectives  40.2 us (72%)
  Pallas kernels  8.81 us (16%)
  starting transfers between devices  6.2 us (11%)
    all_to_all x1, blocking collectives, local(): lax.all_to_all(terms.reshape(128, 8, LANES), ('chip', 'tp'), split_axis=0...  21.1 us
    all_to_all x1, blocking collectives, local(): lax.all_to_all(packed.reshape(32, 24, LANES), 'chip', split_axis=0, conca...  19.1 us
    pallas_call x1, Pallas kernels, attend(): pl.pallas_call(attend_kernel, out_shape=jax.ShapeDtypeStruct((16, 48, LAN...  6.2 us
    ppermute x1, starting transfers between devices, local(): other = lax.ppermute(out_weight, 'core', [(0, 1), (1, 0)])  3.33 us
    ppermute x1, starting transfers between devices, local(): other_part = lax.ppermute(part, 'core', [(0, 1), (1, 0)])  2.87 us
  transfers between devices with their start and end apart: 2, of which 0 were waited for; matrix products, arithmetic and copies ran while one was open for 0% of the time, Pallas kernels for 2%

profile of v3, /device:TPU:1, one launch (start us, length us, event | category | flops | bytes accessed | tf_op | source)
XLA Modules:
  0.0 55.3 jit_solution(14229062456580324060)
XLA Ops:
  0.0 0.0 copy-start
  0.0 6.2 %shard_map.73 = bf16[16,48,128]{2,1,0:T(8,128)(2,1)} custom-call(s32[16]{0:T(128)} %lengths_hbm.1, bf16[16,32,128]{2,1,0:T(8,128)(2,1)} %query_hbm.1, bf16[16,1024,128]{2,1,0:T(8,128)(2,1)} %bitcast.9, bf16[16,1024,128]{2,1,0:T(8,128)(2,1)} %bitcast.10), custom_call_target="tpu_custom_call" | custom-call | flops 270000000 | bytes 8800000 | tf_op jit(solution)/shard_map/pallas_call | solution.py:230
  6.2 0.0 copy-done
  6.2 3.3 %collective-permute-start.1 = (bf16[32,2,16384]{2,1,0:T(2,128)(2,1)S(1)}, bf16[32,2,16384]{2,1,0:T(2,128)(2,1)S(1)}, u32[]{:S(2)}, u32[]{:S(2)}) collective-permute-start(bf16[32,2,16384]{2,1,0:T(2,128)(2,1)S(1)} %copy-done), channel_id=1, source_target_pairs={{0,4},{4,0},{1,5},{5,1},{2,6},{6,2},{3,7},{7,3},{8,12},{12,8},{9,1... | collective-permute-start | bytes 6291464 | tf_op jit(solution)/shard_map/ppermute | solution.py:281
  9.6 19.1 %all_to_all.10 = bf16[32,24,128]{2,1,0:T(8,128)(2,1)S(1)} all-to-all(bf16[32,24,128]{2,1,0:T(8,128)(2,1)} %bitcast.11), channel_id=1, replica_groups=mesh['chip'=32,'core'=2,'tp'=4] {'chip'}, dimensions={0} | all-to-all | bytes 393216 | tf_op jit(solution)/shard_map/all_to_all | solution.py:278
  28.7 0.1 shard_map.74.own_ref
  28.8 0.0 copy-start.1
  28.8 0.0 copy-start.2
  28.8 2.9 %collective-permute-start = (f32[32,128]{1,0:T(8,128)S(1)}, f32[32,128]{1,0:T(8,128)S(1)}, u32[]{:S(2)}, u32[]{:S(2)}) collective-permute-start(f32[32,128]{1,0:T(8,128)S(1)} %shard_map.74.own_ref), channel_id=1, source_target_pairs={{0,4},{4,0},{1,5},{5,1},{2,6},{6,2},{3,7},{7,3},{8,12},{12,8},{9,1... | collective-permute-start | bytes 49160 | tf_op jit(solution)/shard_map/ppermute | solution.py:285
  31.7 0.0 collective-permute-done.1.other_ref
  31.7 1.1 %shard_map.75.weight_ref = bf16[128,8192]{1,0:T(8,128)(2,1)S(1)} custom-call(bf16[32,2,16384]{2,1,0:T(2,128)(2,1)S(1)} %copy-done, bf16[32,2,16384]{2,1,0:T(2,128)(2,1)S(1)} %collective-permute-done.1.other_ref), custom_call_target="tpu_custom_call" | custom-call | bytes 4194304 | tf_op jit(solution)/shard_map/pallas_call | solution.py:265
  32.8 0.0 collective-permute-done.other_ref
  32.8 0.0 copy-done.1
  32.8 0.0 copy-done.2
  32.8 0.7 %shard_map.76 = bf16[64,16,128]{2,1,0:T(8,128)(2,1)S(1)} custom-call(f32[32,128]{1,0:T(8,128)S(1)} %shard_map.74.own_ref, f32[32,128]{1,0:T(8,128)S(1)} %collective-permute-done.other_ref, bf16[128,8192]{1,0:T(8,128)(2,1)S(1)} %shard_map.75.weight_ref, bf16[512,128]{1,0:T(8,128)(2,1)S(1)} %copy-done.1, bf16[64,16]{1,0:T(8,128)(2,1)S(1)} %copy-done.2), custom_call_target="tpu_custom_call" | custom-call | flops 34000000 | bytes 3000000 | tf_op jit(solution)/shard_map/pallas_call | solution.py:97
  33.5 21.1 %all_to_all.11 = bf16[128,8,128]{2,1,0:T(8,128)(2,1)S(1)} all-to-all(bf16[128,8,128]{2,1,0:T(8,128)(2,1)S(1)} %bitcast.6), channel_id=1, replica_groups=mesh['chip'=32,'core'=2,'tp'=4] {'chip','tp'}, dimensions={0} | all-to-all | bytes 524288 | tf_op jit(solution)/shard_map/all_to_all | solution.py:287
  54.6 0.7 %shard_map.77 = bf16[16,64]{1,0:T(8,128)(2,1)} custom-call(bf16[64,16,128]{2,1,0:T(8,128)(2,1)S(1)} %bitcast.7), custom_call_target="tpu_custom_call" | custom-call | flops 131072 | bytes 264192 | tf_op jit(solution)/shard_map/pallas_call | solution.py:121
Async XLA Ops:
  0.0 6.2 %copy-start = (bf16[32,2,16384]{2,1,0:T(2,128)(2,1)S(1)}, bf16[32,2,16384]{2,1,0:T(2,128)(2,1)}, u32[]{:S(2)}) copy-start(bf16[32,2,16384]{2,1,0:T(2,128)(2,1)} %own_ref) | copy-start | bytes 6291460
  6.2 25.5 %collective-permute-start.1 = (bf16[32,2,16384]{2,1,0:T(2,128)(2,1)S(1)}, bf16[32,2,16384]{2,1,0:T(2,128)(2,1)S(1)}, u32[]{:S(2)}, u32[]{:S(2)}) collective-permute-start(bf16[32,2,16384]{2,1,0:T(2,128)(2,1)S(1)} %copy-done), channel_id=1, source_target_pairs={{0,4},{4,0},{1,5},{5,1},{2,6},{6,2},{3,7},{7,3},{8,12},{12,8},{9,1... | collective-permute-start | bytes 6291464 | tf_op jit(solution)/shard_map/ppermute | solution.py:281
  28.8 4.0 %copy-start.1 = (bf16[512,128]{1,0:T(8,128)(2,1)S(1)}, bf16[512,128]{1,0:T(8,128)(2,1)}, u32[]{:S(2)}) copy-start(bf16[512,128]{1,0:T(8,128)(2,1)} %constant.4.clone.spread_ref) | copy-start | bytes 393220
  28.8 4.0 %copy-start.2 = (bf16[64,16]{1,0:T(8,128)(2,1)S(1)}, bf16[64,16]{1,0:T(8,128)(2,1)}, u32[]{:S(2)}) copy-start(bf16[64,16]{1,0:T(8,128)(2,1)} %constant.5.clone.repeat_ref) | copy-start | bytes 6148
  28.8 4.0 %collective-permute-start = (f32[32,128]{1,0:T(8,128)S(1)}, f32[32,128]{1,0:T(8,128)S(1)}, u32[]{:S(2)}, u32[]{:S(2)}) collective-permute-start(f32[32,128]{1,0:T(8,128)S(1)} %shard_map.74.own_ref), channel_id=1, source_target_pairs={{0,4},{4,0},{1,5},{5,1},{2,6},{6,2},{3,7},{7,3},{8,12},{12,8},{9,1... | collective-permute-start | bytes 49160 | tf_op jit(solution)/shard_map/ppermute | solution.py:285

commit v4 on v3

--- a/solution.py
+++ b/solution.py
@@ -151,18 +151,21 @@
     lengths_copy = pltpu.make_async_copy(lengths_hbm, lengths_ref, small_sem.at[1])
     key_copies = []
     value_copies = []
-    for b in range(SEQS):
-        key_copies.append(pltpu.make_async_copy(key_hbm.at[b], keys.at[b], key_sem.at[b]))
-        value_copies.append(pltpu.make_async_copy(value_hbm.at[b], values.at[b], value_sem.at[b]))
+    for t in range(GROUPS):
+        rows = pl.ds(PER * t, PER)
+        key_copies.append(pltpu.make_async_copy(key_hbm.at[rows], keys.at[rows], key_sem.at[t]))
+        value_copies.append(
+            pltpu.make_async_copy(value_hbm.at[rows], values.at[rows], value_sem.at[t])
+        )
     query_copy.start()
     lengths_copy.start()
     loads = []
     for t in range(GROUPS + 1):
         if t < GROUPS:
-            loads.append(key_copies[PER * t : PER * t + PER])
+            loads.append(key_copies[t])
         if t > 0:
-            loads.append(value_copies[PER * t - PER : PER * t])
-    for copy in sum(loads[:AHEAD], []):
+            loads.append(value_copies[t - 1])
+    for copy in loads[:AHEAD]:
         copy.start()
     begun, used = AHEAD, 0
 
@@ -178,12 +181,12 @@
         first = range(PER * t, PER * t + PER) if t < GROUPS else ()
         second = range(PER * (t - 1), PER * t) if 1 <= t <= GROUPS else ()
         third = range(PER * (t - 2), PER * (t - 1)) if t >= 2 else ()
-        for b in first:
-            key_copies[b].wait()
-        for b in third:
-            value_copies[b].wait()
+        if first:
+            key_copies[t].wait()
+        if third:
+            value_copies[t - 2].wait()
         used += (len(first) + len(third)) // PER
-        for copy in sum(loads[begun : used + AHEAD], []):
+        for copy in loads[begun : used + AHEAD]:
             copy.start()
         begun = max(begun, used + AHEAD)
         for b in first:

time: 55.5 us -> 55 us (level)
  no operation moved by 1% of the time
where the time goes in v4:
time: 55 us; the launch traced here: 54.8 us
  blocking collectives  40.2 us (73%)
  Pallas kernels  8.29 us (15%)
  starting transfers between devices  6.19 us (11%)
    all_to_all x1, blocking collectives, local(): lax.all_to_all(terms.reshape(128, 8, LANES), ('chip', 'tp'), split_axis=0...  21.1 us
    all_to_all x1, blocking collectives, local(): lax.all_to_all(packed.reshape(32, 24, LANES), 'chip', split_axis=0, conca...  19.1 us
    pallas_call x1, Pallas kernels, attend(): pl.pallas_call(attend_kernel, out_shape=jax.ShapeDtypeStruct((16, 48, LAN...  5.69 us
    ppermute x1, starting transfers between devices, local(): other = lax.ppermute(out_weight, 'core', [(0, 1), (1, 0)])  3.33 us
    ppermute x1, starting transfers between devices, local(): other_part = lax.ppermute(part, 'core', [(0, 1), (1, 0)])  2.87 us
  transfers between devices with their start and end apart: 2, of which 0 were waited for; matrix products, arithmetic and copies ran while one was open for 0% of the time, Pallas kernels for 2%

profile of v4, /device:TPU:1, one launch (start us, length us, event | category | flops | bytes accessed | tf_op | source)
XLA Modules:
  0.0 54.8 jit_solution(15494560176503425799)
XLA Ops:
  0.0 0.0 copy-start
  0.0 5.7 %shard_map.73 = bf16[16,48,128]{2,1,0:T(8,128)(2,1)} custom-call(s32[16]{0:T(128)} %lengths_hbm.1, bf16[16,32,128]{2,1,0:T(8,128)(2,1)} %query_hbm.1, bf16[16,1024,128]{2,1,0:T(8,128)(2,1)} %bitcast.9, bf16[16,1024,128]{2,1,0:T(8,128)(2,1)} %bitcast.10), custom_call_target="tpu_custom_call" | custom-call | flops 270000000 | bytes 8800000 | tf_op jit(solution)/shard_map/pallas_call | solution.py:233
  5.7 0.0 copy-done
  5.7 3.3 %collective-permute-start.1 = (bf16[32,2,16384]{2,1,0:T(2,128)(2,1)S(1)}, bf16[32,2,16384]{2,1,0:T(2,128)(2,1)S(1)}, u32[]{:S(2)}, u32[]{:S(2)}) collective-permute-start(bf16[32,2,16384]{2,1,0:T(2,128)(2,1)S(1)} %copy-done), channel_id=1, source_target_pairs={{0,4},{4,0},{1,5},{5,1},{2,6},{6,2},{3,7},{7,3},{8,12},{12,8},{9,1... | collective-permute-start | bytes 6291464 | tf_op jit(solution)/shard_map/ppermute | solution.py:284
  9.0 19.1 %all_to_all.10 = bf16[32,24,128]{2,1,0:T(8,128)(2,1)S(1)} all-to-all(bf16[32,24,128]{2,1,0:T(8,128)(2,1)} %bitcast.11), channel_id=1, replica_groups=mesh['chip'=32,'core'=2,'tp'=4] {'chip'}, dimensions={0} | all-to-all | bytes 393216 | tf_op jit(solution)/shard_map/all_to_all | solution.py:281
  28.2 0.1 shard_map.74.own_ref
  28.3 0.0 copy-start.1
  28.3 0.0 copy-start.2
  28.3 2.9 %collective-permute-start = (f32[32,128]{1,0:T(8,128)S(1)}, f32[32,128]{1,0:T(8,128)S(1)}, u32[]{:S(2)}, u32[]{:S(2)}) collective-permute-start(f32[32,128]{1,0:T(8,128)S(1)} %shard_map.74.own_ref), channel_id=1, source_target_pairs={{0,4},{4,0},{1,5},{5,1},{2,6},{6,2},{3,7},{7,3},{8,12},{12,8},{9,1... | collective-permute-start | bytes 49160 | tf_op jit(solution)/shard_map/ppermute | solution.py:288
  31.2 0.0 collective-permute-done.1.other_ref
  31.2 1.1 %shard_map.75.weight_ref = bf16[128,8192]{1,0:T(8,128)(2,1)S(1)} custom-call(bf16[32,2,16384]{2,1,0:T(2,128)(2,1)S(1)} %copy-done, bf16[32,2,16384]{2,1,0:T(2,128)(2,1)S(1)} %collective-permute-done.1.other_ref), custom_call_target="tpu_custom_call" | custom-call | bytes 4194304 | tf_op jit(solution)/shard_map/pallas_call | solution.py:268
  32.3 0.0 collective-permute-done.other_ref
  32.3 0.0 copy-done.1
  32.3 0.0 copy-done.2
  32.3 0.7 %shard_map.76 = bf16[64,16,128]{2,1,0:T(8,128)(2,1)S(1)} custom-call(f32[32,128]{1,0:T(8,128)S(1)} %shard_map.74.own_ref, f32[32,128]{1,0:T(8,128)S(1)} %collective-permute-done.other_ref, bf16[128,8192]{1,0:T(8,128)(2,1)S(1)} %shard_map.75.weight_ref, bf16[512,128]{1,0:T(8,128)(2,1)S(1)} %copy-done.1, bf16[64,16]{1,0:T(8,128)(2,1)S(1)} %copy-done.2), custom_call_target="tpu_custom_call" | custom-call | flops 34000000 | bytes 3000000 | tf_op jit(solution)/shard_map/pallas_call | solution.py:97
  33.0 21.1 %all_to_all.11 = bf16[128,8,128]{2,1,0:T(8,128)(2,1)S(1)} all-to-all(bf16[128,8,128]{2,1,0:T(8,128)(2,1)S(1)} %bitcast.6), channel_id=1, replica_groups=mesh['chip'=32,'core'=2,'tp'=4] {'chip','tp'}, dimensions={0} | all-to-all | bytes 524288 | tf_op jit(solution)/shard_map/all_to_all | solution.py:290
  54.1 0.7 %shard_map.77 = bf16[16,64]{1,0:T(8,128)(2,1)} custom-call(bf16[64,16,128]{2,1,0:T(8,128)(2,1)S(1)} %bitcast.7), custom_call_target="tpu_custom_call" | custom-call | flops 131072 | bytes 264192 | tf_op jit(solution)/shard_map/pallas_call | solution.py:121
Async XLA Ops:
  0.0 5.7 %copy-start = (bf16[32,2,16384]{2,1,0:T(2,128)(2,1)S(1)}, bf16[32,2,16384]{2,1,0:T(2,128)(2,1)}, u32[]{:S(2)}) copy-start(bf16[32,2,16384]{2,1,0:T(2,128)(2,1)} %own_ref) | copy-start | bytes 6291460
  5.7 25.5 %collective-permute-start.1 = (bf16[32,2,16384]{2,1,0:T(2,128)(2,1)S(1)}, bf16[32,2,16384]{2,1,0:T(2,128)(2,1)S(1)}, u32[]{:S(2)}, u32[]{:S(2)}) collective-permute-start(bf16[32,2,16384]{2,1,0:T(2,128)(2,1)S(1)} %copy-done), channel_id=1, source_target_pairs={{0,4},{4,0},{1,5},{5,1},{2,6},{6,2},{3,7},{7,3},{8,12},{12,8},{9,1... | collective-permute-start | bytes 6291464 | tf_op jit(solution)/shard_map/ppermute | solution.py:284
  28.3 4.0 %copy-start.1 = (bf16[512,128]{1,0:T(8,128)(2,1)S(1)}, bf16[512,128]{1,0:T(8,128)(2,1)}, u32[]{:S(2)}) copy-start(bf16[512,128]{1,0:T(8,128)(2,1)} %constant.4.clone.spread_ref) | copy-start | bytes 393220
  28.3 4.0 %copy-start.2 = (bf16[64,16]{1,0:T(8,128)(2,1)S(1)}, bf16[64,16]{1,0:T(8,128)(2,1)}, u32[]{:S(2)}) copy-start(bf16[64,16]{1,0:T(8,128)(2,1)} %constant.5.clone.repeat_ref) | copy-start | bytes 6148
  28.3 4.0 %collective-permute-start = (f32[32,128]{1,0:T(8,128)S(1)}, f32[32,128]{1,0:T(8,128)S(1)}, u32[]{:S(2)}, u32[]{:S(2)}) collective-permute-start(f32[32,128]{1,0:T(8,128)S(1)} %shard_map.74.own_ref), channel_id=1, source_target_pairs={{0,4},{4,0},{1,5},{5,1},{2,6},{6,2},{3,7},{7,3},{8,12},{12,8},{9,1... | collective-permute-start | bytes 49160 | tf_op jit(solution)/shard_map/ppermute | solution.py:288

commit v5 on v4

--- a/solution.py
+++ b/solution.py
@@ -14,9 +14,8 @@
 LANES = 128
 CHIP_FEATURES = 4
 HALF = 8192
-PER = 4
+CUTS = (0, 4, 9, 13, 16)
 AHEAD = 4
-GROUPS = SEQS // PER
 
 
 def spread_table():
@@ -149,10 +148,11 @@
     base = block_index * (width // 2)
     query_copy = pltpu.make_async_copy(query_hbm, query_ref, small_sem.at[0])
     lengths_copy = pltpu.make_async_copy(lengths_hbm, lengths_ref, small_sem.at[1])
+    groups = [range(a, b) for a, b in zip(CUTS[:-1], CUTS[1:])]
     key_copies = []
     value_copies = []
-    for t in range(GROUPS):
-        rows = pl.ds(PER * t, PER)
+    for t, group in enumerate(groups):
+        rows = pl.ds(group.start, len(group))
         key_copies.append(pltpu.make_async_copy(key_hbm.at[rows], keys.at[rows], key_sem.at[t]))
         value_copies.append(
             pltpu.make_async_copy(value_hbm.at[rows], values.at[rows], value_sem.at[t])
@@ -160,8 +160,8 @@
     query_copy.start()
     lengths_copy.start()
     loads = []
-    for t in range(GROUPS + 1):
-        if t < GROUPS:
+    for t in range(len(groups) + 1):
+        if t < len(groups):
             loads.append(key_copies[t])
         if t > 0:
             loads.append(value_copies[t - 1])
@@ -176,16 +176,16 @@
     factor = jnp.float32(LANES**-0.5)
     query_copy.wait()
     lengths_copy.wait()
-    scores, weights, tops, totals, stats = {}, {}, {}, {}, [0.0] * 4
-    for t in range(GROUPS + 2):
-        first = range(PER * t, PER * t + PER) if t < GROUPS else ()
-        second = range(PER * (t - 1), PER * t) if 1 <= t <= GROUPS else ()
-        third = range(PER * (t - 2), PER * (t - 1)) if t >= 2 else ()
+    scores, weights, ratios, stats = {}, {}, {}, [0.0] * 4
+    for t in range(len(groups) + 2):
+        first = groups[t] if t < len(groups) else ()
+        second = groups[t - 1] if 1 <= t <= len(groups) else ()
+        third = groups[t - 2] if t >= 2 else ()
         if first:
             key_copies[t].wait()
         if third:
             value_copies[t - 2].wait()
-        used += (len(first) + len(third)) // PER
+        used += (len(first) > 0) + (len(third) > 0)
         for copy in loads[begun : used + AHEAD]:
             copy.start()
         begun = max(begun, used + AHEAD)
@@ -197,26 +197,29 @@
                 preferred_element_type=jnp.float32,
             )
             scores[b] = jnp.where(position < lengths_ref[b] - base, raw, jnp.float32(-1e30))
+        for b in third:
+            summed = jnp.dot(weights[b], values[b], preferred_element_type=jnp.float32)
+            outs[b * HEADS : b * HEADS + HEADS] = summed * ratios[b]
+            k = b // 4
+            if b % 4 == 3:
+                turned[pl.ds(k, LANES, stride=4), :] = outs[k * LANES : k * LANES + LANES].T
         for b in second:
             top = jnp.max(scores[b], axis=1, keepdims=True)
-            weight = jnp.exp((scores[b] - top) * factor)
-            totals[b] = jnp.sum(weight, axis=1, keepdims=True)
-            tops[b] = top * factor
+            weight = jnp.exp2((scores[b] - top) * (factor * jnp.float32(1.4426950408889634)))
+            total = jnp.sum(weight, axis=1, keepdims=True)
             weights[b] = weight.astype(jnp.bfloat16)
-        for b in third:
-            summed = jnp.dot(weights[b], values[b], preferred_element_type=jnp.float32)
-            coarse = (tops[b] + jnp.log(totals[b])).astype(jnp.bfloat16).astype(jnp.float32)
-            fine = totals[b] * jnp.exp(tops[b] - coarse)
+            top = top * factor
+            coarse = (top + jnp.log(total)).astype(jnp.bfloat16).astype(jnp.float32)
+            fine = total * jnp.exp(top - coarse)
             fine = fine.astype(jnp.bfloat16).astype(jnp.float32)
             fine = jnp.where(lengths_ref[b] > base, fine, 0.0)
-            outs[b * HEADS : b * HEADS + HEADS] = summed * (fine / totals[b])
+            ratios[b] = fine / total
             k = b // 4
             stats[b % 4] = jnp.where(
                 lane == k, coarse, jnp.where(lane == k + 4, fine, stats[b % 4])
             )
-            if b % 4 == 3:
-                turned[pl.ds(k, LANES, stride=4), :] = outs[k * LANES : k * LANES + LANES].T
-    packed = jnp.concatenate(stats, axis=0).T[0:8]
+        if t == len(groups):
+            packed = jnp.concatenate(stats, axis=0).T[0:8]
     features = turned[...].reshape(16, 2, 16, LANES)
     packed = jnp.broadcast_to(packed[None], (16, 8, LANES))
     out_ref[...] = jnp.concatenate(

time: 55 us -> 54.8 us (level)
  no operation moved by 1% of the time
where the time goes in v5:
time: 54.8 us; the launch traced here: 54.6 us
  blocking collectives  40.2 us (73%)
  Pallas kernels  8.1 us (15%)
  starting transfers between devices  6.19 us (11%)
    all_to_all x1, blocking collectives, local(): lax.all_to_all(terms.reshape(128, 8, LANES), ('chip', 'tp'), split_axis=0...  21.1 us
    all_to_all x1, blocking collectives, local(): lax.all_to_all(packed.reshape(32, 24, LANES), 'chip', split_axis=0, conca...  19.1 us
    pallas_call x1, Pallas kernels, attend(): pl.pallas_call(attend_kernel, out_shape=jax.ShapeDtypeStruct((16, 48, LAN...  5.5 us
    ppermute x1, starting transfers between devices, local(): other = lax.ppermute(out_weight, 'core', [(0, 1), (1, 0)])  3.33 us
    ppermute x1, starting transfers between devices, local(): other_part = lax.ppermute(part, 'core', [(0, 1), (1, 0)])  2.87 us
  transfers between devices with their start and end apart: 2, of which 0 were waited for; matrix products, arithmetic and copies ran while one was open for 0% of the time, Pallas kernels for 2%

profile of v5, /device:TPU:1, one launch (start us, length us, event | category | flops | bytes accessed | tf_op | source)
XLA Modules:
  0.0 54.6 jit_solution(17627729431446219624)
XLA Ops:
  0.0 0.0 copy-start
  0.0 5.5 %shard_map.73 = bf16[16,48,128]{2,1,0:T(8,128)(2,1)} custom-call(s32[16]{0:T(128)} %lengths_hbm.1, bf16[16,32,128]{2,1,0:T(8,128)(2,1)} %query_hbm.1, bf16[16,1024,128]{2,1,0:T(8,128)(2,1)} %bitcast.9, bf16[16,1024,128]{2,1,0:T(8,128)(2,1)} %bitcast.10), custom_call_target="tpu_custom_call" | custom-call | flops 270000000 | bytes 8800000 | tf_op jit(solution)/shard_map/pallas_call | solution.py:236
  5.5 0.0 copy-done
  5.5 3.3 %collective-permute-start.1 = (bf16[32,2,16384]{2,1,0:T(2,128)(2,1)S(1)}, bf16[32,2,16384]{2,1,0:T(2,128)(2,1)S(1)}, u32[]{:S(2)}, u32[]{:S(2)}) collective-permute-start(bf16[32,2,16384]{2,1,0:T(2,128)(2,1)S(1)} %copy-done), channel_id=1, source_target_pairs={{0,4},{4,0},{1,5},{5,1},{2,6},{6,2},{3,7},{7,3},{8,12},{12,8},{9,1... | collective-permute-start | bytes 6291464 | tf_op jit(solution)/shard_map/ppermute | solution.py:287
  8.8 19.1 %all_to_all.10 = bf16[32,24,128]{2,1,0:T(8,128)(2,1)S(1)} all-to-all(bf16[32,24,128]{2,1,0:T(8,128)(2,1)} %bitcast.11), channel_id=1, replica_groups=mesh['chip'=32,'core'=2,'tp'=4] {'chip'}, dimensions={0} | all-to-all | bytes 393216 | tf_op jit(solution)/shard_map/all_to_all | solution.py:284
  28.0 0.1 shard_map.74.own_ref
  28.1 0.0 copy-start.1
  28.1 0.0 copy-start.2
  28.1 2.9 %collective-permute-start = (f32[32,128]{1,0:T(8,128)S(1)}, f32[32,128]{1,0:T(8,128)S(1)}, u32[]{:S(2)}, u32[]{:S(2)}) collective-permute-start(f32[32,128]{1,0:T(8,128)S(1)} %shard_map.74.own_ref), channel_id=1, source_target_pairs={{0,4},{4,0},{1,5},{5,1},{2,6},{6,2},{3,7},{7,3},{8,12},{12,8},{9,1... | collective-permute-start | bytes 49160 | tf_op jit(solution)/shard_map/ppermute | solution.py:291
  31.0 0.0 collective-permute-done.1.other_ref
  31.0 1.1 %shard_map.75.weight_ref = bf16[128,8192]{1,0:T(8,128)(2,1)S(1)} custom-call(bf16[32,2,16384]{2,1,0:T(2,128)(2,1)S(1)} %copy-done, bf16[32,2,16384]{2,1,0:T(2,128)(2,1)S(1)} %collective-permute-done.1.other_ref), custom_call_target="tpu_custom_call" | custom-call | bytes 4194304 | tf_op jit(solution)/shard_map/pallas_call | solution.py:271
  32.1 0.0 collective-permute-done.other_ref
  32.1 0.0 copy-done.1
  32.1 0.0 copy-done.2
  32.1 0.7 %shard_map.76 = bf16[64,16,128]{2,1,0:T(8,128)(2,1)S(1)} custom-call(f32[32,128]{1,0:T(8,128)S(1)} %shard_map.74.own_ref, f32[32,128]{1,0:T(8,128)S(1)} %collective-permute-done.other_ref, bf16[128,8192]{1,0:T(8,128)(2,1)S(1)} %shard_map.75.weight_ref, bf16[512,128]{1,0:T(8,128)(2,1)S(1)} %copy-done.1, bf16[64,16]{1,0:T(8,128)(2,1)S(1)} %copy-done.2), custom_call_target="tpu_custom_call" | custom-call | flops 34000000 | bytes 3000000 | tf_op jit(solution)/shard_map/pallas_call | solution.py:96
  32.8 21.1 %all_to_all.11 = bf16[128,8,128]{2,1,0:T(8,128)(2,1)S(1)} all-to-all(bf16[128,8,128]{2,1,0:T(8,128)(2,1)S(1)} %bitcast.6), channel_id=1, replica_groups=mesh['chip'=32,'core'=2,'tp'=4] {'chip','tp'}, dimensions={0} | all-to-all | bytes 524288 | tf_op jit(solution)/shard_map/all_to_all | solution.py:293
  53.9 0.7 %shard_map.77 = bf16[16,64]{1,0:T(8,128)(2,1)} custom-call(bf16[64,16,128]{2,1,0:T(8,128)(2,1)S(1)} %bitcast.7), custom_call_target="tpu_custom_call" | custom-call | flops 131072 | bytes 264192 | tf_op jit(solution)/shard_map/pallas_call | solution.py:120
Async XLA Ops:
  0.0 5.5 %copy-start = (bf16[32,2,16384]{2,1,0:T(2,128)(2,1)S(1)}, bf16[32,2,16384]{2,1,0:T(2,128)(2,1)}, u32[]{:S(2)}) copy-start(bf16[32,2,16384]{2,1,0:T(2,128)(2,1)} %own_ref) | copy-start | bytes 6291460
  5.5 25.5 %collective-permute-start.1 = (bf16[32,2,16384]{2,1,0:T(2,128)(2,1)S(1)}, bf16[32,2,16384]{2,1,0:T(2,128)(2,1)S(1)}, u32[]{:S(2)}, u32[]{:S(2)}) collective-permute-start(bf16[32,2,16384]{2,1,0:T(2,128)(2,1)S(1)} %copy-done), channel_id=1, source_target_pairs={{0,4},{4,0},{1,5},{5,1},{2,6},{6,2},{3,7},{7,3},{8,12},{12,8},{9,1... | collective-permute-start | bytes 6291464 | tf_op jit(solution)/shard_map/ppermute | solution.py:287
  28.1 4.0 %copy-start.1 = (bf16[512,128]{1,0:T(8,128)(2,1)S(1)}, bf16[512,128]{1,0:T(8,128)(2,1)}, u32[]{:S(2)}) copy-start(bf16[512,128]{1,0:T(8,128)(2,1)} %constant.4.clone.spread_ref) | copy-start | bytes 393220
  28.1 4.0 %copy-start.2 = (bf16[64,16]{1,0:T(8,128)(2,1)S(1)}, bf16[64,16]{1,0:T(8,128)(2,1)}, u32[]{:S(2)}) copy-start(bf16[64,16]{1,0:T(8,128)(2,1)} %constant.5.clone.repeat_ref) | copy-start | bytes 6148
  28.1 4.0 %collective-permute-start = (f32[32,128]{1,0:T(8,128)S(1)}, f32[32,128]{1,0:T(8,128)S(1)}, u32[]{:S(2)}, u32[]{:S(2)}) collective-permute-start(f32[32,128]{1,0:T(8,128)S(1)} %shard_map.74.own_ref), channel_id=1, source_target_pairs={{0,4},{4,0},{1,5},{5,1},{2,6},{6,2},{3,7},{7,3},{8,12},{12,8},{9,1... | collective-permute-start | bytes 49160 | tf_op jit(solution)/shard_map/ppermute | solution.py:291

commit v6 on v5

--- a/solution.py
+++ b/solution.py
@@ -76,7 +76,7 @@
     wide = jnp.concatenate([rows[16 * i : 16 * i + 16] for i in range(4)], axis=1)
     left = jnp.dot(wide, spread_ref[...], preferred_element_type=jnp.float32).astype(jnp.bfloat16)
     low = lax.broadcasted_iota(jnp.int32, (8, LANES), 1) < 64
-    step = 1024
+    step = 2048
     for start in range(0, HALF, step):
         part = jnp.dot(
             left, weight_ref[:, start : start + step], preferred_element_type=jnp.float32

time: 54.8 us -> 54.8 us (level)
  no operation moved by 1% of the time
where the time goes in v6:
time: 54.8 us; the launch traced here: 54.6 us
  blocking collectives  40.2 us (73%)
  Pallas kernels  8.1 us (15%)
  starting transfers between devices  6.19 us (11%)
    all_to_all x1, blocking collectives, local(): lax.all_to_all(terms.reshape(128, 8, LANES), ('chip', 'tp'), split_axis=0...  21.1 us
    all_to_all x1, blocking collectives, local(): lax.all_to_all(packed.reshape(32, 24, LANES), 'chip', split_axis=0, conca...  19.1 us
    pallas_call x1, Pallas kernels, attend(): pl.pallas_call(attend_kernel, out_shape=jax.ShapeDtypeStruct((16, 48, LAN...  5.5 us
    ppermute x1, starting transfers between devices, local(): other = lax.ppermute(out_weight, 'core', [(0, 1), (1, 0)])  3.33 us
    ppermute x1, starting transfers between devices, local(): other_part = lax.ppermute(part, 'core', [(0, 1), (1, 0)])  2.87 us
  transfers between devices with their start and end apart: 2, of which 0 were waited for; matrix products, arithmetic and copies ran while one was open for 0% of the time, Pallas kernels for 2%

profile of v6, /device:TPU:1, one launch (start us, length us, event | category | flops | bytes accessed | tf_op | source)
XLA Modules:
  0.0 54.6 jit_solution(17627729431446219624)
XLA Ops:
  0.0 0.0 copy-start
  0.0 5.5 %shard_map.73 = bf16[16,48,128]{2,1,0:T(8,128)(2,1)} custom-call(s32[16]{0:T(128)} %lengths_hbm.1, bf16[16,32,128]{2,1,0:T(8,128)(2,1)} %query_hbm.1, bf16[16,1024,128]{2,1,0:T(8,128)(2,1)} %bitcast.9, bf16[16,1024,128]{2,1,0:T(8,128)(2,1)} %bitcast.10), custom_call_target="tpu_custom_call" | custom-call | flops 270000000 | bytes 8800000 | tf_op jit(solution)/shard_map/pallas_call | solution.py:236
  5.5 0.0 copy-done
  5.5 3.3 %collective-permute-start.1 = (bf16[32,2,16384]{2,1,0:T(2,128)(2,1)S(1)}, bf16[32,2,16384]{2,1,0:T(2,128)(2,1)S(1)}, u32[]{:S(2)}, u32[]{:S(2)}) collective-permute-start(bf16[32,2,16384]{2,1,0:T(2,128)(2,1)S(1)} %copy-done), channel_id=1, source_target_pairs={{0,4},{4,0},{1,5},{5,1},{2,6},{6,2},{3,7},{7,3},{8,12},{12,8},{9,1... | collective-permute-start | bytes 6291464 | tf_op jit(solution)/shard_map/ppermute | solution.py:287
  8.8 19.1 %all_to_all.10 = bf16[32,24,128]{2,1,0:T(8,128)(2,1)S(1)} all-to-all(bf16[32,24,128]{2,1,0:T(8,128)(2,1)} %bitcast.11), channel_id=1, replica_groups=mesh['chip'=32,'core'=2,'tp'=4] {'chip'}, dimensions={0} | all-to-all | bytes 393216 | tf_op jit(solution)/shard_map/all_to_all | solution.py:284
  28.0 0.1 shard_map.74.own_ref
  28.1 0.0 copy-start.1
  28.1 0.0 copy-start.2
  28.1 2.9 %collective-permute-start = (f32[32,128]{1,0:T(8,128)S(1)}, f32[32,128]{1,0:T(8,128)S(1)}, u32[]{:S(2)}, u32[]{:S(2)}) collective-permute-start(f32[32,128]{1,0:T(8,128)S(1)} %shard_map.74.own_ref), channel_id=1, source_target_pairs={{0,4},{4,0},{1,5},{5,1},{2,6},{6,2},{3,7},{7,3},{8,12},{12,8},{9,1... | collective-permute-start | bytes 49160 | tf_op jit(solution)/shard_map/ppermute | solution.py:291
  31.0 0.0 collective-permute-done.1.other_ref
  31.0 1.1 %shard_map.75.weight_ref = bf16[128,8192]{1,0:T(8,128)(2,1)S(1)} custom-call(bf16[32,2,16384]{2,1,0:T(2,128)(2,1)S(1)} %copy-done, bf16[32,2,16384]{2,1,0:T(2,128)(2,1)S(1)} %collective-permute-done.1.other_ref), custom_call_target="tpu_custom_call" | custom-call | bytes 4194304 | tf_op jit(solution)/shard_map/pallas_call | solution.py:271
  32.1 0.0 collective-permute-done.other_ref
  32.1 0.0 copy-done.1
  32.1 0.0 copy-done.2
  32.1 0.7 %shard_map.76 = bf16[64,16,128]{2,1,0:T(8,128)(2,1)S(1)} custom-call(f32[32,128]{1,0:T(8,128)S(1)} %shard_map.74.own_ref, f32[32,128]{1,0:T(8,128)S(1)} %collective-permute-done.other_ref, bf16[128,8192]{1,0:T(8,128)(2,1)S(1)} %shard_map.75.weight_ref, bf16[512,128]{1,0:T(8,128)(2,1)S(1)} %copy-done.1, bf16[64,16]{1,0:T(8,128)(2,1)S(1)} %copy-done.2), custom_call_target="tpu_custom_call" | custom-call | flops 34000000 | bytes 3000000 | tf_op jit(solution)/shard_map/pallas_call | solution.py:96
  32.8 21.1 %all_to_all.11 = bf16[128,8,128]{2,1,0:T(8,128)(2,1)S(1)} all-to-all(bf16[128,8,128]{2,1,0:T(8,128)(2,1)S(1)} %bitcast.6), channel_id=1, replica_groups=mesh['chip'=32,'core'=2,'tp'=4] {'chip','tp'}, dimensions={0} | all-to-all | bytes 524288 | tf_op jit(solution)/shard_map/all_to_all | solution.py:293
  53.9 0.7 %shard_map.77 = bf16[16,64]{1,0:T(8,128)(2,1)} custom-call(bf16[64,16,128]{2,1,0:T(8,128)(2,1)S(1)} %bitcast.7), custom_call_target="tpu_custom_call" | custom-call | flops 131072 | bytes 264192 | tf_op jit(solution)/shard_map/pallas_call | solution.py:120
Async XLA Ops:
  0.0 5.5 %copy-start = (bf16[32,2,16384]{2,1,0:T(2,128)(2,1)S(1)}, bf16[32,2,16384]{2,1,0:T(2,128)(2,1)}, u32[]{:S(2)}) copy-start(bf16[32,2,16384]{2,1,0:T(2,128)(2,1)} %own_ref) | copy-start | bytes 6291460
  5.5 25.5 %collective-permute-start.1 = (bf16[32,2,16384]{2,1,0:T(2,128)(2,1)S(1)}, bf16[32,2,16384]{2,1,0:T(2,128)(2,1)S(1)}, u32[]{:S(2)}, u32[]{:S(2)}) collective-permute-start(bf16[32,2,16384]{2,1,0:T(2,128)(2,1)S(1)} %copy-done), channel_id=1, source_target_pairs={{0,4},{4,0},{1,5},{5,1},{2,6},{6,2},{3,7},{7,3},{8,12},{12,8},{9,1... | collective-permute-start | bytes 6291464 | tf_op jit(solution)/shard_map/ppermute | solution.py:287
  28.1 4.0 %copy-start.1 = (bf16[512,128]{1,0:T(8,128)(2,1)S(1)}, bf16[512,128]{1,0:T(8,128)(2,1)}, u32[]{:S(2)}) copy-start(bf16[512,128]{1,0:T(8,128)(2,1)} %constant.4.clone.spread_ref) | copy-start | bytes 393220
  28.1 4.0 %copy-start.2 = (bf16[64,16]{1,0:T(8,128)(2,1)S(1)}, bf16[64,16]{1,0:T(8,128)(2,1)}, u32[]{:S(2)}) copy-start(bf16[64,16]{1,0:T(8,128)(2,1)} %constant.5.clone.repeat_ref) | copy-start | bytes 6148
  28.1 4.0 %collective-permute-start = (f32[32,128]{1,0:T(8,128)S(1)}, f32[32,128]{1,0:T(8,128)S(1)}, u32[]{:S(2)}, u32[]{:S(2)}) collective-permute-start(f32[32,128]{1,0:T(8,128)S(1)} %shard_map.74.own_ref), channel_id=1, source_target_pairs={{0,4},{4,0},{1,5},{5,1},{2,6},{6,2},{3,7},{7,3},{8,12},{12,8},{9,1... | collective-permute-start | bytes 49160 | tf_op jit(solution)/shard_map/ppermute | solution.py:291
